TPU v7x, 32 devices: a whole 2x2x4 slice. The times are simulated.
32 devices in a mesh: seq: 8 (over y, x, core), head: 4 (over z).
Axes of the slice: x: 2, y: 2, z: 4, core: 2. Of those that a mesh axis runs over, the one named last changes fastest.
Arguments:
- hidden_states: bfloat16 [4, 4096, 768], P(None, 'seq'), may hold values from -6 to 6
- segment_ids: int32 [4, 4096], replicated, may hold values from 0 to 2, as said below
- norm_gain: float32 [768], replicated, may hold values from 0.5 to 1.5
- gate_weight: bfloat16 [768, 1536], P(None, 'head'), may hold values from -0.21875 to 0.21875
- value_weight: bfloat16 [768, 1536], P(None, 'head'), may hold values from -0.21875 to 0.21875
- state_weight: bfloat16 [768, 256], replicated, may hold values from -0.21875 to 0.21875
- step_weight: bfloat16 [768, 24], P(None, 'head'), may hold values from -0.21875 to 0.21875
- kernel_value: float32 [4, 1536], P(None, 'head'), may hold values from -0.6 to 0.6
- kernel_state: float32 [4, 256], replicated, may hold values from -0.6 to 0.6
- bias_value: float32 [1536], P('head'), may hold values from -0.5 to 0.5
- bias_state: float32 [256], replicated, may hold values from -0.5 to 0.5
- step_bias: float32 [24], P('head'), may hold values from -3 to 0
- decay_log: float32 [24], P('head'), may hold values from -10.8 to -0.7
- skip_gain: float32 [24], P('head'), may hold values from 0.5 to 1.5
- inner_gain: float32 [1536], P('head'), may hold values from 0.5 to 1.5
- output_weight: bfloat16 [1536, 768], P('head'), may hold values from -0.15625 to 0.15625
- cotangent: bfloat16 [4, 4096, 768], P(None, 'seq'), may hold values from -6 to 6
Outputs:
- block_output: bfloat16 [4, 4096, 768], P(None, 'seq')
- input_gradient: float32 [4, 4096, 768], P(None, 'seq')
- grad_norm_gain: float32 [768], replicated
- grad_gate_weight: float32 [768, 1536], P(None, 'head')
- grad_value_weight: float32 [768, 1536], P(None, 'head')
- grad_state_weight: float32 [768, 256], replicated
- grad_step_weight: float32 [768, 24], P(None, 'head')
- grad_kernel_value: float32 [4, 1536], P(None, 'head')
- grad_kernel_state: float32 [4, 256], replicated
- grad_bias_value: float32 [1536], P('head')
- grad_bias_state: float32 [256], replicated
- grad_step_bias: float32 [24], P('head')
- grad_decay_log: float32 [24], P('head')
- grad_skip_gain: float32 [24], P('head')
- grad_inner_gain: float32 [1536], P('head')
- grad_output_weight: float32 [1536, 768], P('head')
Inputs may be any that keep to these rules, and one draw needn't show every extreme that they name: `segment_ids`: in every row the ids never fall and take 0, 1, 2 in this order: 0 covers the first 1 to 255 tokens, 2 the last 1 to 255, and 1 all the others.
All inputs are finite; a program needn't handle non-finite values.
Results may differ from a plain program's by a relative error of at most 0.015.
The roundings to bfloat16 on the way count: a program that leaves them out, or rounds other values in their place, can miss the bound.
Values may be sent and summed in bfloat16 or wider, within the bound.
No kernel may reach another device: no remote copies, remote signals or barrier semaphores. Data moves between devices by JAX's collectives and lax.ppermute only.
A program may use at most 192 MiB of HBM per device.

v0:
```python
import jax
import jax.numpy as jnp
from jax import lax
from jax.sharding import PartitionSpec as P

HEADDIM = 64
STATE = 128
BLOCK = 256
INNER = 1536


EPSILON = 1e-05
HIGHEST = lax.Precision.HIGHEST


def from_behind(value, axis, steps):
    count = lax.axis_size(axis)
    first, last = (max(0, -steps), min(count, count - steps))
    return lax.ppermute(value, axis, [(source, source + steps) for source in range(first, last)])


def prefix(x, axis, combine, identity):
    size, place = (lax.axis_size(axis), lax.axis_index(axis))
    everything = jax.tree.map(
        lambda part, kind: lax.all_gather(part.astype(kind), axis), x, (jnp.bfloat16, jnp.bfloat16)
    )
    start = jax.tree.map(
        lambda part, zero: jnp.broadcast_to(jnp.asarray(zero, part.dtype), part.shape), x, identity
    )

    def prefix_step(k, before):
        reached = k < place
        new = combine(
            before, jax.tree.map(lambda part, own: part[k].astype(own.dtype), everything, x)
        )
        return jax.tree.map(lambda a, b: jnp.where(reached, a, b), new, before)

    return lax.fori_loop(0, size, prefix_step, start)


def carried_in(x, axis, combine, identity):
    size, place = (lax.axis_size(axis), lax.axis_index(axis))
    everything = jax.tree.map(
        lambda part, kind: lax.all_gather(part.astype(kind), axis),
        x,
        jax.tree.map(lambda a: jnp.bfloat16 if a.dtype == jnp.float32 else a.dtype, x),
    )
    start = jax.tree.map(
        lambda part, zero: jnp.broadcast_to(jnp.asarray(zero, part.dtype), part.shape), x, identity
    )

    def carried_step(k, before):
        at = size - 1 - k
        reached = at > place
        new = combine(
            before, jax.tree.map(lambda part, own: part[at].astype(own.dtype), everything, x)
        )
        return jax.tree.map(lambda a, b: jnp.where(reached, a, b), new, before)

    return lax.fori_loop(0, size, carried_step, start)


def silu_of(values):
    return values * jax.nn.sigmoid(values)


def silu_slope(values):
    sigmoid = jax.nn.sigmoid(values)
    return sigmoid * (1.0 + values * (1.0 - sigmoid))


def block_step(carried_pair, pieces):
    carried, last_segment = carried_pair
    value_block, write_block, read_block, decay_block, step_block, segment_block = pieces
    running = jnp.cumsum(decay_block, axis=0)
    positions = jnp.arange(BLOCK)
    linked = (segment_block[:, None] == segment_block[None, :]) & (
        positions[:, None] >= positions[None, :]
    )
    linked_float = linked.astype(jnp.float32)[:, :, None]
    spread = jnp.where(linked[:, :, None], running[:, None, :] - running[None, :, :], 0.0)
    scores = jnp.dot(read_block, write_block.T, precision=HIGHEST)
    weights = scores[:, :, None] * jnp.exp(spread) * linked_float * step_block[None, :, :]
    output = jnp.einsum("tsh,shp->thp", weights, value_block, precision=HIGHEST)
    joined = (segment_block == last_segment).astype(jnp.float32)[:, None] * jnp.exp(running)
    output = output + joined[:, :, None] * jnp.einsum(
        "tn,hpn->thp", read_block, carried, precision=HIGHEST
    )
    final_segment = segment_block[BLOCK - 1]
    toward = (
        (segment_block == final_segment).astype(jnp.float32)[:, None]
        * jnp.exp(running[BLOCK - 1][None, :] - running)
        * step_block
    )
    keep_rate = (final_segment == last_segment).astype(jnp.float32) * jnp.exp(running[BLOCK - 1])
    carried = keep_rate[:, None, None] * carried + jnp.einsum(
        "sh,shp,sn->hpn", toward, value_block, write_block, precision=HIGHEST
    )
    return ((carried, final_segment), output)


def block_row(act_rows, step_raw, step_bias, decay_log, skip_gain, segments, before):
    length = act_rows.shape[0]
    head_count = step_bias.shape[0]
    inner_width = head_count * HEADDIM
    values = act_rows[:, :inner_width].reshape(length, head_count, HEADDIM)
    writers = act_rows[:, inner_width : inner_width + STATE]
    readers = act_rows[:, inner_width + STATE :]
    step_size = jax.nn.softplus(step_raw + step_bias)
    log_decay = -step_size * jnp.exp(decay_log)
    block_count = length // BLOCK
    pieces = (
        values.reshape(block_count, BLOCK, head_count, HEADDIM),
        writers.reshape(block_count, BLOCK, STATE),
        readers.reshape(block_count, BLOCK, STATE),
        log_decay.reshape(block_count, BLOCK, head_count),
        step_size.reshape(block_count, BLOCK, head_count),
        segments.reshape(block_count, BLOCK),
    )
    initial = (jnp.zeros((head_count, HEADDIM, STATE), jnp.float32), before)
    (end_state, unused_segment), outputs = lax.scan(jax.checkpoint(block_step), initial, pieces)
    scanned = outputs.reshape(length, head_count, HEADDIM) + skip_gain[None, :, None] * values
    running = jnp.cumsum(log_decay, axis=0)
    linked = (segments == before).astype(jnp.float32)[:, None]
    reading = readers[:, None, :] * (linked * jnp.exp(running))[:, :, None]
    passing = (segments[length - 1] == before).astype(jnp.float32) * jnp.exp(running[length - 1])
    return (scanned.reshape(length, inner_width), end_state, passing, reading)


def forward_combine(earlier, later):
    return (earlier[0] * later[0], later[0][:, :, None, None] * earlier[1] + later[1])


def backward_combine(earlier, later):
    return (later[0] * earlier[0], later[1] + later[0][:, :, None, None] * earlier[1])


def shards(
    hidden_states,
    segment_ids,
    norm_gain,
    gate_weight,
    value_weight,
    state_weight,
    step_weight,
    kernel_value,
    kernel_state,
    bias_value,
    bias_state,
    step_bias,
    decay_log,
    skip_gain,
    inner_gain,
    output_weight,
    cotangent,
):
    row_count, length, model_width = hidden_states.shape
    inner_width = gate_weight.shape[1]
    head_count = step_bias.shape[0]
    tap_count = kernel_value.shape[0]
    seq_index = lax.axis_index("seq")
    head_index = lax.axis_index("head")
    hidden = hidden_states.astype(jnp.float32)
    norm_scale = lax.rsqrt(jnp.mean(hidden * hidden, axis=2, keepdims=True) + EPSILON)
    unit_rows = hidden * norm_scale
    normed = (unit_rows * norm_gain).astype(jnp.bfloat16)
    gate_pre = jnp.einsum("btd,dk->btk", normed, gate_weight, preferred_element_type=jnp.float32)
    inner_values = jnp.einsum(
        "btd,dk->btk", normed, value_weight, preferred_element_type=jnp.float32
    )
    inner_states = jnp.einsum(
        "btd,dk->btk", normed, state_weight, preferred_element_type=jnp.float32
    )
    step_raw = jnp.einsum("btd,dk->btk", normed, step_weight, preferred_element_type=jnp.float32)
    mixed_in = jnp.concatenate([inner_values, inner_states], axis=2).astype(jnp.bfloat16)
    edge_rows = from_behind(mixed_in[:, length - (tap_count - 1) :], "seq", 1)
    padded_segments = jnp.concatenate(
        [jnp.full((row_count, tap_count - 1), -1, jnp.int32), segment_ids], axis=1
    )
    segment_window = lax.dynamic_slice_in_dim(
        padded_segments, seq_index * length, length + tap_count - 1, 1
    )
    segments = segment_window[:, tap_count - 1 :]
    before = segment_window[:, tap_count - 2]
    kernel = jnp.concatenate([kernel_value, kernel_state], axis=1)
    shift_bias = jnp.concatenate([bias_value, bias_state])
    masks = [
        (segment_window[:, offset : offset + length] == segments).astype(jnp.float32)[:, :, None]
        for offset in range(tap_count)
    ]

    def convolve(padded, taps_kernel, taps_bias):
        summed = taps_bias[None, None, :]
        for offset in range(tap_count):
            summed = (
                summed + taps_kernel[offset] * padded[:, offset : offset + length] * masks[offset]
            )
        return silu_of(summed)

    padded_in = jnp.concatenate([edge_rows, mixed_in], axis=1).astype(jnp.float32)
    activated_full, convolve_pull = jax.vjp(convolve, padded_in, kernel, shift_bias)
    activated = lax.optimization_barrier(activated_full.astype(jnp.bfloat16)).astype(jnp.float32)

    def scan_local(act_rows, step_rows, bias_rows, decay_rows, skip_rows):
        mapped = jax.vmap(block_row, in_axes=(0, 0, None, None, None, 0, 0))
        return mapped(act_rows, step_rows, bias_rows, decay_rows, skip_rows, segments, before)

    (scan_open, end_state, passing, reading), scan_pull = jax.vjp(
        scan_local, activated, step_raw, step_bias, decay_log, skip_gain
    )
    unused_rate, start_state = prefix(
        (passing, end_state),
        "seq",
        forward_combine,
        (jnp.ones_like(passing), jnp.zeros_like(end_state)),
    )
    scan_carry = jnp.einsum("btkn,bkpn->btkp", reading, start_state, precision=HIGHEST).reshape(
        row_count, length, inner_width
    )
    scanned = scan_open + scan_carry
    gate_act = silu_of(gate_pre)
    gated = scanned * gate_act
    square_sum = lax.psum(jnp.sum(gated * gated, axis=2), "head")
    gate_scale = lax.rsqrt(square_sum / INNER + EPSILON)[:, :, None]
    gate_unit = gated * gate_scale
    out_in = (gate_unit * inner_gain).astype(jnp.bfloat16)
    partial_out = jnp.einsum(
        "btk,kd->btd", out_in, output_weight, preferred_element_type=jnp.float32
    )
    branch = lax.psum(partial_out.astype(jnp.bfloat16), "head").astype(jnp.float32)
    block_output = (hidden + branch).astype(jnp.bfloat16)
    cot_rows = cotangent.astype(jnp.float32)
    grad_output_weight = jnp.einsum(
        "btk,btd->kd", out_in, cotangent, preferred_element_type=jnp.float32
    )
    grad_out_in = jnp.einsum(
        "btd,kd->btk", cotangent, output_weight, preferred_element_type=jnp.float32
    )
    grad_inner_gain = jnp.sum(grad_out_in * gate_unit, axis=(0, 1))
    grad_unit_gate = grad_out_in * inner_gain
    inner_product = lax.psum(jnp.sum(grad_unit_gate * gated, axis=2), "head")
    grad_gated = (
        gate_scale * grad_unit_gate - gated * gate_scale**3 * (inner_product / INNER)[:, :, None]
    )
    grad_scanned = grad_gated * gate_act
    grad_gate = (grad_gated * scanned * silu_slope(gate_pre)).astype(jnp.bfloat16)
    grad_heads = grad_scanned.reshape(row_count, length, head_count, HEADDIM)
    grad_start = jnp.einsum("btkn,btkp->bkpn", reading, grad_heads, precision=HIGHEST)
    grad_reading = jnp.einsum("btkp,bkpn->btkn", grad_heads, start_state, precision=HIGHEST)
    unused_back, grad_next = carried_in(
        (passing, grad_start),
        "seq",
        backward_combine,
        (jnp.ones_like(passing), jnp.zeros_like(grad_start)),
    )
    grad_passing = jnp.sum(grad_next * start_state, axis=(2, 3))
    grad_act, grad_step_raw, grad_step_bias, grad_decay_log, grad_skip_gain = scan_pull(
        (grad_scanned, grad_next, grad_passing, grad_reading)
    )
    grad_padded, grad_kernel, grad_shift_bias = convolve_pull(grad_act)
    edge_back = from_behind(grad_padded[:, : tap_count - 1], "seq", -1)
    grad_mixed = grad_padded[:, tap_count - 1 :] + jnp.pad(
        edge_back, ((0, 0), (length - tap_count + 1, 0), (0, 0))
    )
    grad_values_in = grad_mixed[:, :, :inner_width].astype(jnp.bfloat16)
    grad_states_in = grad_mixed[:, :, inner_width:].astype(jnp.bfloat16)
    grad_step_in = grad_step_raw.astype(jnp.bfloat16)
    grad_gate_weight = jnp.einsum(
        "btd,btk->dk", normed, grad_gate, preferred_element_type=jnp.float32
    )
    grad_value_weight = jnp.einsum(
        "btd,btk->dk", normed, grad_values_in, preferred_element_type=jnp.float32
    )
    grad_state_weight = jnp.einsum(
        "btd,btk->dk", normed, grad_states_in, preferred_element_type=jnp.float32
    )
    grad_step_weight = jnp.einsum(
        "btd,btk->dk", normed, grad_step_in, preferred_element_type=jnp.float32
    )
    grad_normed = (
        jnp.einsum("btk,dk->btd", grad_gate, gate_weight, preferred_element_type=jnp.float32)
        + jnp.einsum(
            "btk,dk->btd", grad_values_in, value_weight, preferred_element_type=jnp.float32
        )
        + jnp.einsum(
            "btk,dk->btd", grad_states_in, state_weight, preferred_element_type=jnp.float32
        )
        + jnp.einsum("btk,dk->btd", grad_step_in, step_weight, preferred_element_type=jnp.float32)
    )
    grad_unit_all = lax.psum(grad_normed.astype(jnp.bfloat16), "head").astype(jnp.float32)
    grad_gain_rows = jnp.sum(grad_unit_all * unit_rows, axis=(0, 1))
    grad_unit = grad_unit_all * norm_gain
    input_gradient = (
        cot_rows
        + norm_scale * grad_unit
        - hidden * norm_scale**3 * jnp.mean(grad_unit * hidden, axis=2, keepdims=True)
    )
    grad_norm_gain = grad_gain_rows * (head_index == 0).astype(jnp.float32)
    (
        grad_gate_weight,
        grad_value_weight,
        grad_step_weight,
        grad_kernel_value,
        grad_bias_value,
        grad_step_bias,
        grad_decay_log,
        grad_skip_gain,
        grad_inner_gain,
        grad_output_weight,
    ) = (
        lax.psum(grad_gate_weight.astype(jnp.bfloat16), "seq").astype(jnp.float32),
        lax.psum(grad_value_weight.astype(jnp.bfloat16), "seq").astype(jnp.float32),
        lax.psum(grad_step_weight.astype(jnp.bfloat16), "seq").astype(jnp.float32),
        lax.psum(grad_kernel[:, :inner_width].astype(jnp.bfloat16), "seq").astype(jnp.float32),
        lax.psum(grad_shift_bias[:inner_width].astype(jnp.bfloat16), "seq").astype(jnp.float32),
        lax.psum(grad_step_bias.astype(jnp.bfloat16), "seq").astype(jnp.float32),
        lax.psum(grad_decay_log.astype(jnp.bfloat16), "seq").astype(jnp.float32),
        lax.psum(grad_skip_gain.astype(jnp.bfloat16), "seq").astype(jnp.float32),
        lax.psum(grad_inner_gain.astype(jnp.bfloat16), "seq").astype(jnp.float32),
        lax.psum(grad_output_weight.astype(jnp.bfloat16), "seq").astype(jnp.float32),
    )
    grad_norm_gain, grad_state_weight, grad_kernel_state, grad_bias_state = lax.psum(
        (
            grad_norm_gain,
            grad_state_weight,
            grad_kernel[:, inner_width:],
            grad_shift_bias[inner_width:],
        ),
        ("seq", "head"),
    )
    return (
        block_output,
        input_gradient,
        grad_norm_gain,
        grad_gate_weight,
        grad_value_weight,
        grad_state_weight,
        grad_step_weight,
        grad_kernel_value,
        grad_kernel_state,
        grad_bias_value,
        grad_bias_state,
        grad_step_bias,
        grad_decay_log,
        grad_skip_gain,
        grad_inner_gain,
        grad_output_weight,
    )


def solution(mesh):
    placed = (
        P(None, "seq", None),
        P(),
        P(),
        P(None, "head"),
        P(None, "head"),
        P(),
        P(None, "head"),
        P(None, "head"),
        P(),
        P("head"),
        P(),
        P("head"),
        P("head"),
        P("head"),
        P("head"),
        P("head", None),
        P(None, "seq", None),
    )
    return jax.shard_map(
        shards,
        mesh=mesh,
        in_specs=placed,
        out_specs=(
            P(None, "seq", None),
            P(None, "seq", None),
            P(),
            P(None, "head"),
            P(None, "head"),
            P(),
            P(None, "head"),
            P(None, "head"),
            P(),
            P("head"),
            P(),
            P("head"),
            P("head"),
            P("head"),
            P("head"),
            P("head", None),
        ),
        check_vma=False,
    )
```

profile of v0, /device:TPU:0, one launch (start us, length us, event | category | flops | bytes accessed | tf_op | source)
XLA Modules:
  0.0 1083.5 jit_solution(8765804803998819148)
XLA Ops:
  56.1 58.4 %while.75 = (s32[]{:T(128)}, f32[4,6,64,128]{3,2,1,0:T(8,128)S(1)}, s32[4]{0:T(128)S(1)}, f32[2,4,256,6,64]{2,4,3,1,0:T(8,128)}, f32[2,4,6,64,128]{4,3,2,1,0:T(8...) while((s32[]{:T(128)}, f32[4,6,64,128]{3,2,1,0:T(8,128)S(1)}, ...), condition=%wide.region_4.5_spmd.clone, body=%wide.region_1.4_spmd.clone.sunk | while | flops 2830266368 | bytes 44843940 | solution.py:121
  67.6 7.9 fusion.305
  96.8 7.9 fusion.305
  115.4 19.7 %reduce-window.78 = f32[4,6,4,128]{3,2,1,0:T(4,128)S(1)} reduce-window(f32[4,6,4,128]{3,2,1,0:T(4,128)S(1)} %reshape.644, f32[]{:T(128)} %constant.202.clone.1), window={size=1x1x1x128 pad=0_0x0_0x0_0x127_0}, to_apply=%region_5.6 | reduce-window | flops 1560576 | bytes 98308 | tf_op jit(solution)/shard_map/reduce-window.6
  136.6 10.0 all_gather.18
  161.3 9.8 while.76
  182.1 12.1 %psum.126 = f32[4,512]{1,0:T(4,128)S(1)} all-reduce(f32[4,512]{1,0:T(4,128)S(1)} %get-tuple-element.1073), channel_id=1, replica_groups=mesh['seq'=8,'head'=4] {'head'}, use_global_device_ids=true, to_apply=%region_10.11 | all-reduce | flops 2048 | bytes 16384 | tf_op jit(solution)/shard_map/psum | solution.py:223
  200.8 8.5 psum.128
  209.3 8.4 multiply_reduce_fusion.9
  258.2 9.8 while.77
  274.7 264.2 %while.74 = (s32[]{:T(128)}, f32[4,6,64,128]{3,2,1,0:T(8,128)S(1)}, f32[2,4,256,6,64]{2,4,3,1,0:T(8,128)}, f32[2,4,256,128]{3,2,1,0:T(8,128)}, f32[2,4,256,128]{...) while((s32[]{:T(128)}, f32[4,6,64,128]{3,2,1,0:T(8,128)S(1)}, ...), condition=%wide.region_29.30_spmd, body=%wide.region_17.29_spmd.sunk | while | flops 6682112000 | bytes 89413752 | solution.py:121
  325.4 12.7 %fusion.284 = (f32[4,256,6]{1,2,0:T(8,128)}, f32[4,256,6]{1,2,0:T(8,128)}, f32[4,256,6]{1,2,0:T(8,128)S(1)}, f32[4,256,256]{2,1,0:T(8,128)}) fusion(f32[4,256,6]{1,2,0:T(8,128)S(1)} %copy.771, f32[4,256,256]{2,1,0:T(8,128)} %get-tuple-element.1379, f32[4,256,6]{1,2,0:T(8,128)} %copy.777, f32[4,256,256]{2,1,0:T(8,128)} %fusion.283, ...), kind=kOutput, calls=%fused_computation.17.clone.1 | convolution fusion | flops 1231271936 | bytes 6676480 | tf_op jit(solution)/shard_map/transpose(jvp(vmap()))/while/body/eval_jaxpr/checkpoint/tsh,shp->thp/dot_general | solution.py:84
  354.7 30.2 %reduce-window.96 = f32[4,6,2,128]{3,2,1,0:T(2,128)S(1)} reduce-window(f32[4,6,2,128]{3,2,1,0:T(2,128)S(1)} %copy.786, f32[]{:T(128)} %constant.202.clone.1..sunk), window={size=1x1x1x128 pad=0_0x0_0x0_0x0_127}, to_apply=%region_26.26 | reduce-window | flops 780288 | bytes 49156 | tf_op jit(solution)/shard_map/reduce-window.36
  444.5 12.7 %fusion.284 = (f32[4,256,6]{1,2,0:T(8,128)}, f32[4,256,6]{1,2,0:T(8,128)}, f32[4,256,6]{1,2,0:T(8,128)S(1)}, f32[4,256,256]{2,1,0:T(8,128)}) fusion(f32[4,256,6]{1,2,0:T(8,128)S(1)} %copy.771, f32[4,256,256]{2,1,0:T(8,128)} %get-tuple-element.1379, f32[4,256,6]{1,2,0:T(8,128)} %copy.777, f32[4,256,256]{2,1,0:T(8,128)} %fusion.283, ...), kind=kOutput, calls=%fused_computation.17.clone.1 | convolution fusion | flops 1231271936 | bytes 6676480 | tf_op jit(solution)/shard_map/transpose(jvp(vmap()))/while/body/eval_jaxpr/checkpoint/tsh,shp->thp/dot_general | solution.py:84
  473.7 30.2 %reduce-window.96 = f32[4,6,2,128]{3,2,1,0:T(2,128)S(1)} reduce-window(f32[4,6,2,128]{3,2,1,0:T(2,128)S(1)} %copy.786, f32[]{:T(128)} %constant.202.clone.1..sunk), window={size=1x1x1x128 pad=0_0x0_0x0_0x0_127}, to_apply=%region_26.26 | reduce-window | flops 780288 | bytes 49156 | tf_op jit(solution)/shard_map/reduce-window.36
  563.5 30.2 %reduce-window.80 = f32[4,6,4,128]{3,2,1,0:T(4,128)S(1)} reduce-window(f32[4,6,4,128]{3,2,1,0:T(4,128)S(1)} %reshape.646, f32[]{:T(128)} %constant.202.clone.1), window={size=1x1x1x128 pad=0_0x0_0x0_0x0_127}, to_apply=%region_32.33 | reduce-window | flops 1560576 | bytes 98308 | tf_op jit(solution)/shard_map/reduce-window.8
  597.0 14.6 %multiply_reduce_fusion.7 = (f32[640]{0:T(1024)S(1)}, f32[640]{0:T(1024)S(1)}, f32[640]{0:T(1024)S(1)}, f32[640]{0:T(1024)S(1)}, f32[640]{0:T(1024)S(1)}, /*index=5*/f32[4,512,640]{1,2,0:T(8,128)S(1)}) fusion(f32[4,515,640]{1,2,0:T(8,128)} %copy-done.2, f32[4,512]{1,0:T(4,128)S(1)} %copy-done.54, f32[4,512]{1,0:T(4,128)S(1)} %copy-done.56, ...), kind=kLoop, calls=%fused_computation.189 | loop fusion | flops 30143360 | bytes 36737536 | tf_op jit(solution)/shard_map/transpose(jvp())/reduce_sum | solution.py:196
  627.4 10.6 pad_add_fusion
  652.0 9.3 add_convert_fusion
  665.1 24.4 %all-reduce.17 = (bf16[768,6]{0,1:T(8,128)(2,1)S(1)}, bf16[4,384]{1,0:T(4,128)(2,1)S(1)}, bf16[384]{0:T(512)(128)(2,1)S(1)}, bf16[6]{0:T(256)(128)(2,1)S(1)}, bf...) all-reduce(bf16[768,6]{0,1:T(8,128)(2,1)S(1)} %fusion.137, ...), channel_id=1, replica_groups=mesh['seq'=8,'head'=4] {'seq'}, use_global_device_ids=true, to_apply=%region_41.42 | all-reduce | flops 6930 | bytes 27720 | tf_op jit(solution)/shard_map/psum | solution.py:313
  697.7 16.9 %all-reduce.26.cloned.1.call-done = (bf16[768,384]{1,0:T(8,128)(2,1)}, bf16[768,384]{1,0:T(8,128)(2,1)}, bf16[384,768]{1,0:T(8,128)(2,1)}) async-done(((bf16[768,384]{1,0:T(8,128)(2,1)}, bf16[768,384]{1,0:T(8,128)(2,1)}, bf16[384,768]{1,0:T(8,128)(2,1)}), (bf16[768,384]{1,0:T(8,128)(2,1)}, bf16[768,384]{1,0:T(8,128)(2,1)}, bf16[384,768]{1,0:T(8,128)(2,1)})) %all-reduce.26.cloned.1.call-update) | async-done | bytes 1769488 | tf_op jit(solution)/shard_map/psum | solution.py:311
  720.0 219.9 %all-reduce.28.cloned.1.call-done = (bf16[4,512,768]{2,1,0:T(8,128)(2,1)}, bf16[4,512,768]{2,1,0:T(8,128)(2,1)}) async-done(((bf16[4,512,768]{2,1,0:T(8,128)(2,1)}, bf16[4,512,768]{2,1,0:T(8,128)(2,1)}), (bf16[4,512,768]{2,1,0:T(8,128)(2,1)}, bf16[4,512,768]{2,1,0:T(8,128)(2,1)})) %all-reduce.28.cloned.1.call-update) | async-done | bytes 6291472 | tf_op jit(solution)/shard_map/psum | solution.py:230
  952.0 39.4 %all-reduce.16 = (f32[768]{0:T(1024)}, f32[4,256]{1,0:T(4,128)}, f32[256]{0:T(256)}) all-reduce(f32[768]{0:T(1024)S(1)} %broadcast_multiply_fusion.4, f32[4,256]{1,0:T(4,128)S(1)} %pad_add_fusion.3, f32[256]{0:T(256)S(1)} %slice.207), channel_id=1, replica_groups=mesh['seq'=8,'head'=4] {'seq','head'}, use_global_device_ids=true, to_apply=%region_37.38 | all-reduce | flops 2048 | bytes 16384 | tf_op jit(solution)/shard_map/psum | solution.py:322
  991.4 83.0 %all-reduce.24.cloned.1.call-done = f32[768,256]{1,0:T(8,128)} async-done(((f32[768,256]{1,0:T(8,128)}), f32[768,256]{1,0:T(8,128)}) %all-reduce.24.cloned.1.call-update) | async-done | bytes 786448 | tf_op jit(solution)/shard_map/psum | solution.py:322
  (609 shorter events, 432.0 us)
Async XLA Ops:
  7.2 167.9 %copy-start = (bf16[768,384]{1,0:T(8,128)(2,1)S(1)}, bf16[768,384]{1,0:T(8,128)(2,1)}, u32[]{:S(2)}) copy-start(bf16[768,384]{1,0:T(8,128)(2,1)} %param.28) | copy-start | bytes 1769476
  7.2 154.1 %all-gather.5.cloned.1.call-start = ((), (), s32[]{:S(2)}) async-start(), calls=%async_computation.1 | async-start | bytes 3538944 | tf_op jit(solution)/shard_map/all_gather | solution.py:25
  10.6 244.2 %copy-start.57 = (f32[4,512]{1,0:T(4,128)}, f32[4,512]{1,0:T(4,128)S(1)}, u32[]{:S(2)}) copy-start(f32[4,512]{1,0:T(4,128)S(1)} %get-tuple-element.1117) | copy-start | bytes 24580
  16.0 8.6 collective-permute-start
  23.7 122.8 %copy-start.59 = (f32[4,512]{1,0:T(4,128)}, f32[4,512]{1,0:T(4,128)S(1)}, u32[]{:S(2)}) copy-start(f32[4,512]{1,0:T(4,128)S(1)} %get-tuple-element.1076) | copy-start | bytes 24580
  56.1 59.3 %copy-start.61 = (f32[4,6,512]{2,1,0:T(8,128)S(1)}, f32[4,6,512]{2,1,0:T(8,128)}, u32[]{:S(2)}) copy-start(f32[4,6,512]{2,1,0:T(8,128)} %get-tuple-element.1120) | copy-start | bytes 147460
  56.1 79.6 %copy-start.96 = (f32[6]{0:T(128)S(1)}, f32[6]{0:T(128)}, u32[]{:S(2)}) copy-start(f32[6]{0:T(128)} %param.38) | copy-start | bytes 76
  56.1 79.7 %copy-start.38 = (s32[4,4096]{1,0:T(4,128)S(1)}, s32[4,4096]{1,0:T(4,128)}, u32[]{:S(2)}) copy-start(s32[4,4096]{1,0:T(4,128)} %param.26) | copy-start | bytes 196612
  56.1 79.7 %copy-start.86 = (s32[4,1]{1,0:T(4,128)S(1)}, s32[4,1]{1,0:T(4,128)}, u32[]{:S(2)}) copy-start(s32[4,1]{1,0:T(4,128)} %get-tuple-element.1081) | copy-start | bytes 52
  115.3 142.9 %all-gather.7.cloned.1.call-start = ((), (), s32[]{:S(2)}) async-start(), calls=%async_computation.2 | async-start | bytes 3538944 | tf_op jit(solution)/shard_map/all_gather | solution.py:44
  135.8 39.2 %copy-start.83 = (f32[384]{0:T(512)}, f32[384]{0:T(512)S(1)}, u32[]{:S(2)}) copy-start(f32[384]{0:T(512)S(1)} %mul.949) | copy-start | bytes 4612
  175.1 19.1 %copy-start.42 = (bf16[384,768]{1,0:T(8,128)(2,1)S(1)}, bf16[384,768]{1,0:T(8,128)(2,1)}, u32[]{:S(2)}) copy-start(bf16[384,768]{1,0:T(8,128)(2,1)} %param.40) | copy-start | bytes 1769476
  227.1 487.5 %all-reduce.26.cloned.1.call-start = ((), (), s32[]{:S(2)}) async-start(), calls=%async_computation.3 | async-start | bytes 3538944 | tf_op jit(solution)/shard_map/psum | solution.py:311
  307.6 30.5 %copy-start.62 = (f32[4]{0:T(128)}, f32[4]{0:T(128)S(1)}, u32[]{:S(2)}) copy-start(f32[4]{0:T(128)S(1)} %compare_convert_fusion.13) | copy-start | bytes 52 | tf_op jit(solution)/shard_map/transpose(jvp(vmap()))/while
  426.7 30.5 %copy-start.62 = (f32[4]{0:T(128)}, f32[4]{0:T(128)S(1)}, u32[]{:S(2)}) copy-start(f32[4]{0:T(128)S(1)} %compare_convert_fusion.13) | copy-start | bytes 52 | tf_op jit(solution)/shard_map/transpose(jvp(vmap()))/while
  557.7 36.4 %copy-start.50 = (f32[2,4,256,6]{2,1,3,0:T(4,128)S(1)}, f32[2,4,256,6]{2,1,3,0:T(4,128)}, u32[]{:S(2)}) copy-start(f32[2,4,256,6]{2,1,3,0:T(4,128)} %get-tuple-element.692) | copy-start | bytes 147460
  557.7 38.1 %copy-start.34 = (f32[4,512,128]{1,2,0:T(8,128)S(1)}, f32[4,512,128]{1,2,0:T(8,128)}, u32[]{:S(2)}) copy-start(f32[4,512,128]{1,2,0:T(8,128)} %get-tuple-element.966) | copy-start | bytes 3145732
  563.1 33.9 %copy-start.52 = (f32[4,512]{1,0:T(4,128)S(1)}, f32[4,512]{1,0:T(4,128)}, u32[]{:S(2)}) copy-start(f32[4,512]{1,0:T(4,128)} %copy-done.51) | copy-start | bytes 24580
  563.1 33.9 %copy-start.54 = (f32[4,512]{1,0:T(4,128)S(1)}, f32[4,512]{1,0:T(4,128)}, u32[]{:S(2)}) copy-start(f32[4,512]{1,0:T(4,128)} %copy-done.53) | copy-start | bytes 24580
  563.1 33.9 %copy-start.56 = (f32[4,512]{1,0:T(4,128)S(1)}, f32[4,512]{1,0:T(4,128)}, u32[]{:S(2)}) copy-start(f32[4,512]{1,0:T(4,128)} %copy-done.55) | copy-start | bytes 24580
  622.1 15.9 %collective-permute-start.1 = (f32[4,3,640]{2,0,1:T(4,128)S(1)}, f32[4,3,640]{2,0,1:T(4,128)S(1)}, u32[]{:S(2)}, u32[]{:S(2)}) collective-permute-start(f32[4,3,640]{2,0,1:T(4,128)S(1)} %copy.616), channel_id=1, source_target_pairs={{4,0},{8,4},{12,8},{16,12},{20,16},{24,20},{28,24},{5,1},{9,5},{13... | collective-permute-start | bytes 92168 | tf_op jit(solution)/shard_map/ppermute | solution.py:19
  651.9 288.0 %all-reduce.28.cloned.1.call-start = ((), (), s32[]{:S(2)}) async-start(), calls=%async_computation.4 | async-start | bytes 12582912 | tf_op jit(solution)/shard_map/psum | solution.py:230
  661.3 413.2 %all-reduce.24.cloned.1.call-start = ((), (), s32[]{:S(2)}) async-start(), calls=%async_computation | async-start | bytes 1572864 | tf_op jit(solution)/shard_map/psum | solution.py:322
  945.2 131.3 %copy-start.1 = (bf16[768,384]{1,0:T(8,128)(2,1)S(1)}, bf16[768,384]{1,0:T(8,128)(2,1)}, u32[]{:S(2)}) copy-start(bf16[768,384]{1,0:T(8,128)(2,1)} %param.28) | copy-start | bytes 1769476
  (98 other events, 552.8 us)
Sparse Core Ops, SparseCore 0:
  115.4 34.8 all-gather.4
  227.2 31.0 all-gather.6
  652.0 62.4 all-reduce.25
  717.5 222.3 all-reduce.27
  946.4 128.0 all-reduce.23
where the time goes:
time: 1090 us; the launch traced here: 1080 us
  waiting for transfers between devices  320 us (29%)
  other arithmetic  279 us (26%)
  matrix products  205 us (19%)
  local copies, waits for them, and re-layouts  138 us (13%)
  blocking collectives  94.3 us (9%)
  loops' own time  27.5 us (3%)
  between operations  15.4 us (1%)
    psum x1, waiting for transfers between devices, shards(): lax.psum(partial_out.astype(jnp.bfloat16), 'head').astype(jnp.float32)  220 us
    another operation x28, other arithmetic  145 us
    psum x1, waiting for transfers between devices, shards(): lax.psum((grad_norm_gain, grad_state_weight, grad_kernel[:, inner_width:]...  83 us
    dot_general x6, matrix products, block_step(): output = jnp.einsum('tsh,shp->thp', weights, value_block, precision=HIGHEST)  56.9 us
    psum x1, blocking collectives, shards(): lax.psum((grad_norm_gain, grad_state_weight, grad_kernel[:, inner_width:]...  39.4 us
    another operation x2, loops' own time, block_row(): lax.scan(jax.checkpoint(block_step), initial, pieces)  27 us
    dot_general x8, matrix products, block_step(): jnp.einsum('tn,hpn->thp', read_block, carried, precision=HIGHEST)  24.5 us
    psum x1, blocking collectives, shards(): lax.psum(grad_step_weight.astype(jnp.bfloat16), 'seq').astype(jnp.float32)  24.4 us
  transfers between devices with their start and end apart: 7, of which 4 were waited for; matrix products, arithmetic and copies ran while one was open for 12% of the time, Pallas kernels for 0%

commit v1 on v0

v1 whole, which is shorter than its diff:
```python
import jax
import jax.numpy as jnp
from jax import lax
from jax.experimental import pallas as pl
from jax.experimental.pallas import tpu as pltpu
from jax.sharding import PartitionSpec as P

HEADDIM = 64
STATE = 128
EPSILON = 1e-05
HIGHEST = lax.Precision.HIGHEST
LANES = 128
HALO = 16
TILE = 256
BF16 = jnp.bfloat16
F32 = jnp.float32
VMEM_LIMIT = 56 * 1024 * 1024


def bits_of(count):
    return count.bit_length() - 1


def swap(value, axis, bit):
    count = lax.axis_size(axis)
    return lax.ppermute(value, axis, [(i, i ^ (1 << bit)) for i in range(count)])


def bit_of(axis, bit):
    return (lax.axis_index(axis) >> bit) & 1


def joined(mine, other, upper):
    return jnp.where(
        upper == 1,
        jnp.concatenate([other, mine], axis=0),
        jnp.concatenate([mine, other], axis=0),
    )


def seq_rank():
    bits = bits_of(lax.axis_size("seq"))
    return sum(bit_of("seq", b) << (bits - 1 - b) for b in range(bits))


def gather_head(value):
    for b in range(bits_of(lax.axis_size("head"))):
        value = joined(value, swap(value, "head", b), bit_of("head", b))
    return value


def gather_seq(value):
    for b in reversed(range(bits_of(lax.axis_size("seq")))):
        value = joined(value, swap(value, "seq", b), bit_of("seq", b))
    return value


def gather_weight(weight):
    seq_count, head_count = lax.axis_size("seq"), lax.axis_size("head")
    part = weight.shape[0] // seq_count
    own = lax.dynamic_slice_in_dim(weight, seq_rank() * part, part, 0)
    whole = gather_seq(gather_head(own[None]))
    return whole.reshape(seq_count, head_count, part, weight.shape[1])


def halve(value, axis, bit):
    value = value.reshape((2, value.shape[0] // 2) + value.shape[1:])
    upper = bit_of(axis, bit)
    keep = lax.dynamic_index_in_dim(value, upper, 0, keepdims=False)
    send = lax.dynamic_index_in_dim(value, 1 - upper, 0, keepdims=False)
    got = swap(send, axis, bit)
    return (keep.astype(F32) + got.astype(F32)).astype(value.dtype)


def scatter_seq(value):
    for b in range(bits_of(lax.axis_size("seq"))):
        value = halve(value, "seq", b)
    return value


def reduce_weight(grad):
    seq_count, head_count, part, width = grad.shape
    grad = scatter_seq(grad.reshape(seq_count * head_count, part, width))
    for b in reversed(range(bits_of(head_count))):
        grad = halve(grad, "head", b)
    return gather_seq(grad).reshape(seq_count * part, width)


def reduce_all(value):
    value = scatter_seq(value)
    for b in range(bits_of(lax.axis_size("head"))):
        value = (value.astype(F32) + swap(value, "head", b).astype(F32)).astype(value.dtype)
    return gather_seq(value)


def chunk_permute(value, rows, target):
    seq_count, head_count = lax.axis_size("seq"), lax.axis_size("head")
    parts = head_count // rows
    pairs = []
    for s in range(seq_count):
        for h in range(head_count):
            goal = target(s * parts + h % parts)
            if 0 <= goal < seq_count * parts:
                place = (goal // parts) * head_count + (h // parts) * parts + goal % parts
                pairs.append((s * head_count + h, place))
    return lax.ppermute(value, ("seq", "head"), pairs)


def carried(rate, state, rows, chunk, reverse):
    count = lax.axis_size("seq") * (lax.axis_size("head") // rows)
    before = jnp.zeros_like(state)
    before_rate = jnp.ones_like(rate)
    for b in range(bits_of(count)):
        got = chunk_permute(state.astype(BF16), rows, lambda c: c ^ (1 << b)).astype(F32)
        got_rate = chunk_permute(rate, rows, lambda c: c ^ (1 << b))
        after = ((chunk >> b) & 1) == (0 if reverse else 1)
        before = jnp.where(after, before_rate[:, None] * got + before, before)
        before_rate = jnp.where(after, before_rate * got_rate, before_rate)
        if b < bits_of(count) - 1:
            state = jnp.where(
                after, rate[:, None] * got + state, got_rate[:, None] * state + got
            )
            rate = rate * got_rate
    return before


def contract(a, b, dims):
    return lax.dot_general(a, b, ((dims[0], dims[1]), ((), ())), preferred_element_type=F32)


def taps_of(padded, masks):
    taps = []
    for k in range(4):
        moved = padded if k == 3 else pltpu.roll(padded, 3 - k, 0)
        tap = moved[HALO:]
        taps.append(tap if k == 3 else tap * masks[:, k : k + 1])
    return taps


def summed_of(taps, kernel, bias):
    summed = bias
    for k in range(4):
        summed = summed + kernel[k : k + 1, :] * taps[k]
    return summed


def linked_of(seg_col, seg_row):
    length = seg_col.shape[0]
    row = lax.broadcasted_iota(jnp.int32, (length, length), 0)
    col = lax.broadcasted_iota(jnp.int32, (length, length), 1)
    return jnp.where((row >= col) & (seg_col == seg_row), 1.0, 0.0)


def blocks_of(length):
    count = length // TILE
    return [(t, s) for t in range(count) for s in range(t + 1)]


def cut(index):
    return slice(index * TILE, (index + 1) * TILE)


def scan_kernel(
    mixed_ref,
    states_ref,
    kernel_ref,
    bias_ref,
    kernel_state_ref,
    bias_state_ref,
    masks_ref,
    seg_col_ref,
    seg_row_ref,
    step_ref,
    decay_ref,
    x_ref,
    open_ref,
    end_ref,
    run_ref,
    size_ref,
    writers_ref,
    readers_ref,
    turned_ref,
    scores,
    run_all,
    size_all,
):
    pair = pl.program_id(0)
    length = x_ref.shape[0]
    pairs = run_all.shape[0]
    low = lax.broadcasted_iota(jnp.int32, (1, LANES), 1) < HEADDIM
    masks = masks_ref[...]

    @pl.when(pair == 0)
    def _():
        taps = taps_of(states_ref[...].astype(F32), masks)
        summed = summed_of(taps, kernel_state_ref[...], bias_state_ref[...])
        active = (summed * jax.nn.sigmoid(summed)).astype(BF16)
        writers = active[:, :STATE]
        readers = active[:, STATE:]
        writers_ref[...] = writers
        readers_ref[...] = readers
        linked = linked_of(seg_col_ref[...], seg_row_ref[...])
        scores[...] = contract(readers, writers, ((1,), (1,))) * linked
        row = lax.broadcasted_iota(jnp.int32, (length, length), 0)
        col = lax.broadcasted_iota(jnp.int32, (length, length), 1)
        lower = jnp.where(row >= col, 1.0, 0.0)
        run = jnp.dot(lower, decay_ref[...], precision=HIGHEST, preferred_element_type=F32)
        turned_ref[...] = run.T
        size = step_ref[...]
        for i in range(pairs):
            a, b = 2 * i, 2 * i + 1
            run_all[i] = jnp.where(low, run[:, a : a + 1], run[:, b : b + 1])
            size_all[i] = jnp.where(low, size[:, a : a + 1], size[:, b : b + 1])

    run = run_all[pair]
    size = size_all[pair]
    run_ref[...] = run
    size_ref[...] = size
    taps = taps_of(mixed_ref[...].astype(F32), masks)
    summed = summed_of(taps, kernel_ref[...], bias_ref[...])
    x = (summed * jax.nn.sigmoid(summed)).astype(BF16)
    x_ref[...] = x
    sized = x.astype(F32) * size
    sized_low = sized.astype(BF16)
    zero = jnp.zeros((), BF16)
    halves = (jnp.where(low, sized_low, zero), jnp.where(low, zero, sized_low))
    totals = [None] * (length // TILE)
    for t, s in blocks_of(length):
        score = scores[cut(t), cut(s)]
        for j in range(2):
            row = turned_ref[pl.ds(2 * pair + j, 1), :][:, cut(s)]
            col = run[cut(t), j * HEADDIM : j * HEADDIM + 1]
            weight = (score * jnp.exp(jnp.minimum(col - row, 0.0))).astype(BF16)
            part = contract(weight, halves[j][cut(s)], ((1,), (0,)))
            totals[t] = part if totals[t] is None else totals[t] + part
    for t, total in enumerate(totals):
        open_ref[cut(t), :] = total
    seg_col = seg_col_ref[...]
    last = jnp.where(seg_col == seg_col[length - 1 : length, :], 1.0, 0.0)
    toward = last * jnp.exp(run[length - 1 : length, :] - run)
    end_ref[...] = contract((toward * sized).astype(BF16), writers_ref[...], ((0,), (0,)))


def gate_kernel(
    open_ref,
    x_ref,
    run_ref,
    gate_ref,
    grad_out_ref,
    hidden_ref,
    entered_ref,
    readers_ref,
    start_ref,
    weight_ref,
    gain_ref,
    skip_ref,
    total_ref,
    out_in_ref,
    block_ref,
    grad_scan_ref,
    grad_gate_ref,
    grad_read_ref,
    sums_ref,
    grad_start_ref,
):
    step = pl.program_id(0)
    inner = gain_ref.shape[1]
    gain = gain_ref[...]
    x = x_ref[...].astype(F32)
    start = start_ref[...]
    readers = readers_ref[...]
    reach = entered_ref[...] * jnp.exp(run_ref[...])
    total = open_ref[...] + reach * contract(readers, start, ((1,), (1,)))
    total_ref[...] = total
    scanned = total + skip_ref[...] * x
    gate = gate_ref[...]
    sig = jax.nn.sigmoid(gate)
    act = gate * sig
    gated = scanned * act
    scale = lax.rsqrt(jnp.sum(gated * gated, axis=1, keepdims=True) / inner + EPSILON)
    unit = gated * scale
    out_in = (unit * gain).astype(BF16)
    out_in_ref[...] = out_in
    branch = contract(out_in, weight_ref[...], ((1,), (0,)))
    block_ref[...] = (hidden_ref[...].astype(F32) + branch).astype(BF16)
    grad_out = grad_out_ref[...]
    q = grad_out * gain
    inner_product = jnp.sum(q * gated, axis=1, keepdims=True) / inner
    grad_gated = scale * q - gated * (scale * scale * scale * inner_product)
    grad_scan = grad_gated * act
    grad_scan_low = grad_scan.astype(BF16)
    grad_scan_ref[...] = grad_scan_low
    slope = sig * (1.0 + gate * (1.0 - sig))
    grad_gate_ref[...] = (grad_gated * scanned * slope).astype(BF16)
    reached = (reach * grad_scan).astype(BF16)
    grad_read_ref[...] = contract(reached, start, ((1,), (0,)))
    grad_start = contract(reached, readers, ((0,), (0,)))
    gain_sum = jnp.sum(grad_out * unit, axis=0, keepdims=True)
    skip_sum = jnp.sum(grad_scan * x, axis=0, keepdims=True)
    rows = lax.broadcasted_iota(jnp.int32, (8, inner), 0)
    sums = jnp.where(rows == 0, gain_sum, jnp.where(rows == 1, skip_sum, 0.0))

    @pl.when(step == 0)
    def _():
        sums_ref[...] = sums
        grad_start_ref[...] = grad_start

    @pl.when(step > 0)
    def _():
        sums_ref[...] += sums
        grad_start_ref[...] += grad_start


def conv_back(grad_act, padded, kernel, bias, masks):
    length, width = grad_act.shape
    taps = taps_of(padded, masks)
    summed = summed_of(taps, kernel, bias)
    sig = jax.nn.sigmoid(summed)
    grad_u = grad_act * (sig * (1.0 + summed * (1.0 - sig)))
    rows = lax.broadcasted_iota(jnp.int32, (8, width), 0)
    sums = jnp.where(rows == 4, jnp.sum(grad_u, axis=0, keepdims=True), 0.0)
    mixed = None
    nothing = jnp.zeros((HALO, width), F32)
    for k in range(4):
        sums = jnp.where(rows == k, jnp.sum(grad_u * taps[k], axis=0, keepdims=True), sums)
        back = grad_u * kernel[k : k + 1, :]
        if k < 3:
            back = back * masks[:, k : k + 1]
        back = jnp.concatenate([nothing, back], axis=0)
        if k < 3:
            back = pltpu.roll(back, length + HALO - (3 - k), 0)
        mixed = back if mixed is None else mixed + back
    return mixed, sums


def back_kernel(
    x_ref,
    mixed_ref,
    run_ref,
    size_ref,
    grad_scan_ref,
    total_ref,
    grad_end_ref,
    start_ref,
    kernel_ref,
    bias_ref,
    skip_ref,
    states_ref,
    kernel_state_ref,
    bias_state_ref,
    masks_ref,
    seg_col_ref,
    seg_row_ref,
    writers_ref,
    readers_ref,
    turned_ref,
    grad_read_ref,
    grad_mixed_ref,
    sums_ref,
    grad_states_ref,
    sums_state_ref,
    rate_ref,
    direct_ref,
    scores,
    grad_scores,
    grad_write,
    rate_sum,
    direct_sum,
):
    pair = pl.program_id(0)
    length = x_ref.shape[0]
    low = lax.broadcasted_iota(jnp.int32, (1, LANES), 1) < HEADDIM
    lane = lax.broadcasted_iota(jnp.int32, (1, LANES), 1)
    masks = masks_ref[...]
    writers = writers_ref[...]
    readers = readers_ref[...]
    seg_col = seg_col_ref[...]

    @pl.when(pair == 0)
    def _():
        linked = linked_of(seg_col, seg_row_ref[...])
        scores[...] = contract(readers, writers, ((1,), (1,))) * linked
        grad_scores[...] = jnp.zeros_like(grad_scores)
        grad_write[...] = jnp.zeros_like(grad_write)
        rate_sum[...] = jnp.zeros_like(rate_sum)
        direct_sum[...] = jnp.zeros_like(direct_sum)

    run = run_ref[...]
    size = size_ref[...]
    x = x_ref[...].astype(F32)
    sized = x * size
    sized_low = sized.astype(BF16)
    grad_scan = grad_scan_ref[...]
    zero = jnp.zeros((), BF16)
    halves = (jnp.where(low, grad_scan, zero), jnp.where(low, zero, grad_scan))
    inner = [None] * (length // TILE)
    for t, s in blocks_of(length):
        score = scores[cut(t), cut(s)]
        grad_score = grad_scores[cut(t), cut(s)]
        for j in range(2):
            row = turned_ref[pl.ds(2 * pair + j, 1), :][:, cut(s)]
            col = run[cut(t), j * HEADDIM : j * HEADDIM + 1]
            decay = jnp.exp(jnp.minimum(col - row, 0.0))
            weight = (score * decay).astype(BF16)
            grad_weight = contract(halves[j][cut(t)], sized_low[cut(s)], ((1,), (1,)))
            grad_score = grad_score + grad_weight * decay
            part = contract(weight, halves[j][cut(t)], ((0,), (0,)))
            inner[s] = part if inner[s] is None else inner[s] + part
        grad_scores[cut(t), cut(s)] = grad_score
    inner = inner[0] if len(inner) == 1 else jnp.concatenate(inner, axis=0)
    last = jnp.where(seg_col == seg_col[length - 1 : length, :], 1.0, 0.0)
    toward = last * jnp.exp(run[length - 1 : length, :] - run)
    grad_end = grad_end_ref[...]
    outer = toward * contract(writers, grad_end.astype(BF16), ((1,), (1,)))
    grad_write[...] += contract(
        (toward * sized).astype(BF16), grad_end.astype(BF16), ((1,), (0,))
    )
    grad_sized = inner + outer
    grad_scan = grad_scan.astype(F32)
    sized_low = sized_low.astype(F32)
    change = grad_scan * total_ref[...] - sized_low * grad_sized
    straight = x * grad_sized
    for j in range(2):
        side = low if j == 0 else jnp.logical_not(low)
        here = lane == 2 * pair + j
        one = jnp.sum(jnp.where(side, change, 0.0), axis=1, keepdims=True)
        rate_sum[...] += jnp.where(here, one, 0.0)
        two = jnp.sum(jnp.where(side, straight, 0.0), axis=1, keepdims=True)
        direct_sum[...] += jnp.where(here, two, 0.0)
    grad_x = size * grad_sized + skip_ref[...] * grad_scan
    grad_mixed, sums = conv_back(
        grad_x, mixed_ref[...].astype(F32), kernel_ref[...], bias_ref[...], masks
    )
    grad_mixed_ref[...] = grad_mixed
    rows = lax.broadcasted_iota(jnp.int32, (8, LANES), 0)
    outer_sum = jnp.sum(sized_low * outer, axis=0, keepdims=True)
    kept = start_ref[...].astype(F32) * grad_end
    kept_low = jnp.sum(kept[:HEADDIM], axis=0, keepdims=True)
    kept_high = jnp.sum(kept[HEADDIM:], axis=0, keepdims=True)
    sums = jnp.where(rows == 5, outer_sum, sums)
    sums = jnp.where(rows == 6, kept_low, jnp.where(rows == 7, kept_high, sums))
    sums_ref[...] = sums

    @pl.when(pair == pl.num_programs(0) - 1)
    def _():
        linked = linked_of(seg_col, seg_row_ref[...])
        grad_score = (grad_scores[...] * linked).astype(BF16)
        grad_readers = contract(grad_score, writers, ((1,), (0,))) + grad_read_ref[...]
        grad_writers = contract(grad_score, readers, ((0,), (0,))) + grad_write[...]
        grad_act = jnp.concatenate([grad_writers, grad_readers], axis=1)
        grad_states, state_sums = conv_back(
            grad_act,
            states_ref[...].astype(F32),
            kernel_state_ref[...],
            bias_state_ref[...],
            masks,
        )
        grad_states_ref[...] = grad_states
        sums_state_ref[...] = state_sums
        row = lax.broadcasted_iota(jnp.int32, (length, length), 0)
        col = lax.broadcasted_iota(jnp.int32, (length, length), 1)
        upper = jnp.where(col >= row, 1.0, 0.0)
        rate_ref[...] = jnp.dot(
            upper, rate_sum[...], precision=HIGHEST, preferred_element_type=F32
        )
        direct_ref[...] = direct_sum[...]


def whole_spec(shape):
    return pl.BlockSpec(shape, lambda i: (0,) * len(shape))


def columns_spec(rows):
    return pl.BlockSpec((rows, LANES), lambda i: (0, i))


def rows_spec(rows, width):
    return pl.BlockSpec((rows, width), lambda i: (i, 0))


def run_scan(mixed, states, kernel, bias, kernel_state, bias_state, masks, seg_col, seg_row, step, decay):
    length = mixed.shape[0] - HALO
    inner = mixed.shape[1]
    pairs = inner // LANES
    wide = 2 * STATE
    return pl.pallas_call(
        scan_kernel,
        grid=(pairs,),
        in_specs=[
            columns_spec(length + HALO),
            whole_spec((length + HALO, wide)),
            columns_spec(4),
            columns_spec(1),
            whole_spec((4, wide)),
            whole_spec((1, wide)),
            whole_spec((length, 4)),
            whole_spec((length, 1)),
            whole_spec((1, length)),
            whole_spec((length, LANES)),
            whole_spec((length, LANES)),
        ],
        out_specs=[
            columns_spec(length),
            columns_spec(length),
            rows_spec(LANES, STATE),
            columns_spec(length),
            columns_spec(length),
            whole_spec((length, STATE)),
            whole_spec((length, STATE)),
            whole_spec((LANES, length)),
        ],
        out_shape=[
            jax.ShapeDtypeStruct((length, inner), BF16),
            jax.ShapeDtypeStruct((length, inner), F32),
            jax.ShapeDtypeStruct((inner, STATE), F32),
            jax.ShapeDtypeStruct((length, inner), F32),
            jax.ShapeDtypeStruct((length, inner), F32),
            jax.ShapeDtypeStruct((length, STATE), BF16),
            jax.ShapeDtypeStruct((length, STATE), BF16),
            jax.ShapeDtypeStruct((LANES, length), F32),
        ],
        scratch_shapes=[
            pltpu.VMEM((length, length), F32),
            pltpu.VMEM((pairs, length, LANES), F32),
            pltpu.VMEM((pairs, length, LANES), F32),
        ],
        compiler_params=pltpu.CompilerParams(vmem_limit_bytes=VMEM_LIMIT),
        name="scan_forward",
    )(mixed, states, kernel, bias, kernel_state, bias_state, masks, seg_col, seg_row, step, decay)


def run_gate(opened, x, run, gate, grad_out, hidden, entered, readers, start, weight, gain, skip):
    length, inner = x.shape
    width = hidden.shape[1]
    tile = 128
    return pl.pallas_call(
        gate_kernel,
        grid=(length // tile,),
        in_specs=[
            rows_spec(tile, inner),
            rows_spec(tile, inner),
            rows_spec(tile, inner),
            rows_spec(tile, inner),
            rows_spec(tile, inner),
            rows_spec(tile, width),
            rows_spec(tile, 1),
            rows_spec(tile, STATE),
            whole_spec((inner, STATE)),
            whole_spec((inner, width)),
            whole_spec((1, inner)),
            whole_spec((1, inner)),
        ],
        out_specs=[
            rows_spec(tile, inner),
            rows_spec(tile, inner),
            rows_spec(tile, width),
            rows_spec(tile, inner),
            rows_spec(tile, inner),
            rows_spec(tile, STATE),
            whole_spec((8, inner)),
            whole_spec((inner, STATE)),
        ],
        out_shape=[
            jax.ShapeDtypeStruct((length, inner), F32),
            jax.ShapeDtypeStruct((length, inner), BF16),
            jax.ShapeDtypeStruct((length, width), BF16),
            jax.ShapeDtypeStruct((length, inner), BF16),
            jax.ShapeDtypeStruct((length, inner), BF16),
            jax.ShapeDtypeStruct((length, STATE), F32),
            jax.ShapeDtypeStruct((8, inner), F32),
            jax.ShapeDtypeStruct((inner, STATE), F32),
        ],
        compiler_params=pltpu.CompilerParams(vmem_limit_bytes=VMEM_LIMIT),
        name="gate_both",
    )(opened, x, run, gate, grad_out, hidden, entered, readers, start, weight, gain, skip)


def run_back(
    x, mixed, run, size, grad_scan, total, grad_end, start, kernel, bias, skip,
    states, kernel_state, bias_state, masks, seg_col, seg_row, writers, readers, turned, grad_read,
):
    length, inner = x.shape
    wide = 2 * STATE
    return pl.pallas_call(
        back_kernel,
        grid=(inner // LANES,),
        in_specs=[
            columns_spec(length),
            columns_spec(length + HALO),
            columns_spec(length),
            columns_spec(length),
            columns_spec(length),
            columns_spec(length),
            rows_spec(LANES, STATE),
            rows_spec(LANES, STATE),
            columns_spec(4),
            columns_spec(1),
            columns_spec(1),
            whole_spec((length + HALO, wide)),
            whole_spec((4, wide)),
            whole_spec((1, wide)),
            whole_spec((length, 4)),
            whole_spec((length, 1)),
            whole_spec((1, length)),
            whole_spec((length, STATE)),
            whole_spec((length, STATE)),
            whole_spec((LANES, length)),
            whole_spec((length, STATE)),
        ],
        out_specs=[
            columns_spec(length + HALO),
            columns_spec(8),
            whole_spec((length + HALO, wide)),
            whole_spec((8, wide)),
            whole_spec((length, LANES)),
            whole_spec((length, LANES)),
        ],
        out_shape=[
            jax.ShapeDtypeStruct((length + HALO, inner), F32),
            jax.ShapeDtypeStruct((8, inner), F32),
            jax.ShapeDtypeStruct((length + HALO, wide), F32),
            jax.ShapeDtypeStruct((8, wide), F32),
            jax.ShapeDtypeStruct((length, LANES), F32),
            jax.ShapeDtypeStruct((length, LANES), F32),
        ],
        scratch_shapes=[
            pltpu.VMEM((length, length), F32),
            pltpu.VMEM((length, length), F32),
            pltpu.VMEM((length, STATE), F32),
            pltpu.VMEM((length, LANES), F32),
            pltpu.VMEM((length, LANES), F32),
        ],
        compiler_params=pltpu.CompilerParams(vmem_limit_bytes=VMEM_LIMIT),
        name="scan_backward",
    )(
        x, mixed, run, size, grad_scan, total, grad_end, start, kernel, bias, skip,
        states, kernel_state, bias_state, masks, seg_col, seg_row, writers, readers, turned, grad_read,
    )


def dot(a, b):
    return jnp.dot(a, b, preferred_element_type=F32)


def dot_rows(a, b):
    return lax.dot_general(a, b, (((0,), (0,)), ((), ())), preferred_element_type=F32)


def dot_turned(a, b):
    return lax.dot_general(a, b, (((1,), (1,)), ((), ())), preferred_element_type=F32)


def to_columns(gathered):
    seq_count, head_count, part, width = gathered.shape
    return gathered.transpose(0, 2, 1, 3).reshape(seq_count * part, head_count * width)


def from_columns(grad, head_count):
    seq_count = lax.axis_size("seq")
    rows, columns = grad.shape
    split = grad.astype(BF16).reshape(
        seq_count, rows // seq_count, head_count, columns // head_count
    )
    return split.transpose(0, 2, 1, 3)


def to_rows(gathered):
    seq_count, head_count, part, width = gathered.shape
    return gathered.transpose(1, 0, 2, 3).reshape(seq_count * head_count * part, width)


def from_rows(grad, head_count):
    seq_count = lax.axis_size("seq")
    rows, columns = grad.shape
    split = grad.astype(BF16).reshape(
        head_count, seq_count, rows // (seq_count * head_count), columns
    )
    return split.transpose(1, 0, 2, 3)


def pad_lanes(value):
    return jnp.pad(value, ((0, 0), (0, LANES - value.shape[1])))


def shards(
    hidden_states,
    segment_ids,
    norm_gain,
    gate_weight,
    value_weight,
    state_weight,
    step_weight,
    kernel_value,
    kernel_state,
    bias_value,
    bias_state,
    step_bias,
    decay_log,
    skip_gain,
    inner_gain,
    output_weight,
    cotangent,
):
    rows, block, width = hidden_states.shape
    head_devices = lax.axis_size("head")
    parts = head_devices // rows
    length = block // parts
    seq_index, head_index = lax.axis_index("seq"), lax.axis_index("head")
    row_index, part_index = head_index // parts, head_index % parts
    chunk = seq_index * parts + part_index
    local_inner = gate_weight.shape[1]
    local_heads = step_bias.shape[0]
    inner = local_inner * head_devices
    heads = local_heads * head_devices
    taps = kernel_value.shape[0]

    value_full = to_columns(gather_weight(value_weight))
    gate_full = to_columns(gather_weight(gate_weight))
    output_full = to_rows(gather_weight(output_weight))
    step_full = gather_head(step_weight[None])
    step_full = step_full.transpose(1, 0, 2).reshape(width, heads)
    small = jnp.concatenate(
        [kernel_value.reshape(-1), bias_value, inner_gain, step_bias, decay_log, skip_gain]
    )
    small = gather_head(small[None])
    at = taps * local_inner
    kernel_full = small[:, :at].reshape(head_devices, taps, local_inner)
    kernel_full = kernel_full.transpose(1, 0, 2).reshape(taps, inner)
    bias_full = small[:, at : at + local_inner].reshape(1, inner)
    at += local_inner
    gain_full = small[:, at : at + local_inner].reshape(1, inner)
    at += local_inner
    step_bias_full = small[:, at : at + local_heads].reshape(heads)
    at += local_heads
    decay_full = jnp.exp(small[:, at : at + local_heads].reshape(heads))
    at += local_heads
    skip_full = small[:, at : at + local_heads].reshape(heads)
    skip_wide = jnp.repeat(skip_full, HEADDIM)[None]

    place = (row_index, part_index * length, 0)
    hidden_low = lax.dynamic_slice(hidden_states, place, (1, length, width))[0]
    cot = lax.dynamic_slice(cotangent, place, (1, length, width))[0]
    edge = chunk_permute(hidden_low[length - HALO :], rows, lambda c: c + 1)
    hidden_ext = jnp.concatenate([edge, hidden_low], axis=0).astype(F32)
    scale_ext = lax.rsqrt(jnp.mean(hidden_ext * hidden_ext, axis=1, keepdims=True) + EPSILON)
    normed_ext = (hidden_ext * scale_ext * norm_gain).astype(BF16)
    normed = normed_ext[HALO:]
    hidden = hidden_low.astype(F32)
    norm_scale = scale_ext[HALO:]

    seg_line = lax.dynamic_slice_in_dim(segment_ids, row_index, 1, 0)[0]
    seg_line = jnp.concatenate([jnp.full((HALO,), -1, jnp.int32), seg_line])
    window = lax.dynamic_slice_in_dim(seg_line, chunk * length, length + HALO, 0)
    segments = window[HALO:]
    before = window[HALO - 1]
    masks = jnp.stack(
        [window[HALO - 3 + k : HALO - 3 + k + length] == segments for k in range(taps)], axis=1
    ).astype(F32)
    entered = (segments == before).astype(F32)[:, None]
    seg_col = segments.astype(F32)[:, None]
    seg_row = segments.astype(F32)[None]

    mixed = dot(normed_ext, value_full).astype(BF16)
    states = dot(normed_ext, state_weight).astype(BF16)
    step_raw = dot(normed, step_full) + step_bias_full
    step_size = jax.nn.softplus(step_raw)
    log_decay = -step_size * decay_full
    passing = jnp.exp(jnp.sum(log_decay, axis=0)) * (segments[length - 1] == before).astype(F32)
    passing_wide = jnp.repeat(passing, HEADDIM)

    kernel_rows = kernel_full
    bias_state_row = bias_state[None]
    x, opened, end_state, run, size, writers, readers, turned = run_scan(
        mixed,
        states,
        kernel_rows,
        bias_full,
        kernel_state,
        bias_state_row,
        masks,
        seg_col,
        seg_row,
        pad_lanes(step_size),
        pad_lanes(log_decay),
    )
    start = carried(passing_wide, end_state, rows, chunk, False).astype(BF16)
    gate_pre = dot(normed, gate_full)
    grad_out_in = dot_turned(cot, output_full)
    total, out_in, block_rows, grad_scan, grad_gate, grad_read, gate_sums, grad_start = run_gate(
        opened,
        x,
        run,
        gate_pre,
        grad_out_in,
        hidden_low,
        entered,
        readers,
        start,
        output_full,
        gain_full,
        skip_wide,
    )
    block_output = lax.all_gather(block_rows, "head").reshape(rows, block, width)
    grad_output_weight = reduce_weight(from_rows(dot_rows(out_in, cot), head_devices))
    grad_gate_weight = reduce_weight(from_columns(dot_rows(normed, grad_gate), head_devices))
    grad_end = carried(passing_wide, grad_start, rows, chunk, True)
    grad_mixed, sums, grad_states, state_sums, rate, direct = run_back(
        x,
        mixed,
        run,
        size,
        grad_scan,
        total,
        grad_end,
        start,
        kernel_rows,
        bias_full,
        skip_wide,
        states,
        kernel_state,
        bias_state_row,
        masks,
        seg_col,
        seg_row,
        writers,
        readers,
        turned,
        grad_read,
    )
    edge_values = chunk_permute(grad_mixed[HALO - 8 : HALO], rows, lambda c: c - 1)
    edge_states = chunk_permute(grad_states[HALO - 8 : HALO], rows, lambda c: c - 1)
    fill = ((length - 8, 0), (0, 0))
    grad_values_in = (grad_mixed[HALO:] + jnp.pad(edge_values, fill)).astype(BF16)
    grad_states_in = (grad_states[HALO:] + jnp.pad(edge_states, fill)).astype(BF16)

    kept = jnp.stack([sums[6].reshape(-1, LANES).sum(1), sums[7].reshape(-1, LANES).sum(1)], axis=1)
    rate_end = sums[5].reshape(heads, HEADDIM).sum(1) + passing * kept.reshape(heads)
    grad_log_decay = rate[:, :heads] + rate_end
    grad_step_size = direct[:, :heads] - grad_log_decay * decay_full
    grad_step_raw = grad_step_size * jax.nn.sigmoid(step_raw)
    grad_step_in = grad_step_raw.astype(BF16)
    grad_decay_log = jnp.sum(grad_log_decay * log_decay, axis=0)
    grad_step_bias = jnp.sum(grad_step_raw, axis=0)
    grad_skip_gain = gate_sums[1].reshape(heads, HEADDIM).sum(1)

    grad_normed = (
        dot_turned(grad_gate, gate_full)
        + dot_turned(grad_values_in, value_full)
        + dot_turned(grad_states_in, state_weight)
        + dot_turned(grad_step_in, step_full)
    )
    grad_norm_gain = jnp.sum(grad_normed * hidden * norm_scale, axis=0)
    grad_unit = grad_normed * norm_gain
    change = norm_scale * grad_unit - hidden * norm_scale**3 * jnp.mean(
        grad_unit * hidden, axis=1, keepdims=True
    )
    changes = lax.all_gather(change.astype(BF16), "head").reshape(rows, block, width)
    input_gradient = cotangent.astype(F32) + changes.astype(F32)

    grad_value_weight = reduce_weight(
        from_columns(dot_rows(normed, grad_values_in), head_devices)
    )
    grad_state_weight = dot_rows(normed, grad_states_in)
    grad_step_weight = dot_rows(normed, grad_step_in)
    pieces = [
        grad_state_weight,
        grad_step_weight,
        grad_norm_gain,
        sums[:taps],
        state_sums[:taps],
        sums[4],
        state_sums[4],
        grad_step_bias,
        grad_decay_log,
        grad_skip_gain,
        gate_sums[0],
    ]
    flat = jnp.concatenate([piece.reshape(-1) for piece in pieces]).astype(BF16)
    unit = lax.axis_size("seq") * 16 * LANES
    padded = -(-flat.shape[0] // unit) * unit
    flat = jnp.pad(flat, (0, padded - flat.shape[0])).reshape(-1, LANES)
    flat = reduce_all(flat).reshape(-1).astype(F32)
    summed, at = [], 0
    for piece in pieces:
        summed.append(flat[at : at + piece.size].reshape(piece.shape))
        at += piece.size

    def own(value, axis):
        size = value.shape[axis] // head_devices
        return lax.dynamic_slice_in_dim(value, head_index * size, size, axis)

    return (
        block_output,
        input_gradient,
        summed[2],
        grad_gate_weight.astype(F32),
        grad_value_weight.astype(F32),
        summed[0],
        own(summed[1], 1),
        own(summed[3], 1),
        summed[4],
        own(summed[5], 0),
        summed[6],
        own(summed[7], 0),
        own(summed[8], 0),
        own(summed[9], 0),
        own(summed[10], 0),
        grad_output_weight.astype(F32),
    )


def solution(mesh):
    placed = (
        P(None, "seq", None),
        P(),
        P(),
        P(None, "head"),
        P(None, "head"),
        P(),
        P(None, "head"),
        P(None, "head"),
        P(),
        P("head"),
        P(),
        P("head"),
        P("head"),
        P("head"),
        P("head"),
        P("head", None),
        P(None, "seq", None),
    )
    return jax.shard_map(
        shards,
        mesh=mesh,
        in_specs=placed,
        out_specs=(
            P(None, "seq", None),
            P(None, "seq", None),
            P(),
            P(None, "head"),
            P(None, "head"),
            P(),
            P(None, "head"),
            P(None, "head"),
            P(),
            P("head"),
            P(),
            P("head"),
            P("head"),
            P("head"),
            P("head"),
            P("head", None),
        ),
        check_vma=False,
    )
```

time: 1090 us -> 417 us (0.38)
  other arithmetic: 279 us -> 51.4 us
  waiting for transfers between devices: 320 us -> 107 us
  matrix products: 205 us -> 32.6 us
  blocking collectives: 94.3 us -> 0 us
  local copies, waits for them, and re-layouts: 138 us -> 72.8 us
  starting transfers between devices: 4.11 us -> 69.1 us
  Pallas kernels: 0 us -> 60.5 us
  loops' own time: 27.5 us -> 0 us
    psum x3 -> x0, waiting for transfers between devices: 320 us -> none  [the longest x1 220 us: shards(): lax.psum(partial_out.astype(jnp.bfloat16), 'head').astype(jnp.float32)]
    dot_general x46 -> x14, matrix products: 205 us -> 32.6 us  [the longest x5 14.4 us: dot_turned(): lax.dot_general(a, b, (((1,), (1,)), ((), ())), preferred_element_type=F32)]
    another operation x28 -> x4, other arithmetic: 145 us -> 1.59 us
    ppermute x2 -> x62, waiting for transfers between devices: 0.01 us -> 107 us  [the longest x51 86.8 us: swap(): return lax.ppermute(value, axis, [(i, i ^ 1 << bit) for i in range(count)])]
    psum x4 -> x0, blocking collectives: 84.4 us -> none  [the longest x1 39.4 us: shards(): lax.psum((grad_norm_gain, grad_state_weight, grad_kernel[:, inner_width:]...]
    ppermute x2 -> x62, starting transfers between devices: 3.65 us -> 69 us  [the longest x51 59.2 us: swap(): return lax.ppermute(value, axis, [(i, i ^ 1 << bit) for i in range(count)])]
    pallas_call x0 -> x3, Pallas kernels: none -> 60.5 us  [the longest x1 28.3 us: run_back(): pl.pallas_call(back_kernel, grid=(inner // LANES,), in_specs=[columns_spe...]
    reduce_sum x11 -> x5, other arithmetic: 37.9 us -> 1.77 us  [the longest x1 1.18 us: shards(): grad_step_bias = jnp.sum(grad_step_raw, axis=0)]
  transfers between devices with their start and end apart: 7 -> 64, of which waited for: 4 -> 25; matrix products, arithmetic and copies ran while one was open for 12% -> 33% of each run, Pallas kernels for 0% -> 11%
where the time goes in v1:
time: 417 us; the launch traced here: 411 us
  waiting for transfers between devices  107 us (26%)
  local copies, waits for them, and re-layouts  72.8 us (17%)
  starting transfers between devices  69.1 us (17%)
  Pallas kernels  60.5 us (15%)
  other arithmetic  51.4 us (12%)
  matrix products  32.6 us (8%)
  between operations  17.1 us (4%)
    ppermute x51, waiting for transfers between devices, swap(): return lax.ppermute(value, axis, [(i, i ^ 1 << bit) for i in range(count)])  86.8 us
    ppermute x51, starting transfers between devices, swap(): return lax.ppermute(value, axis, [(i, i ^ 1 << bit) for i in range(count)])  59.2 us
    pallas_call x1, Pallas kernels, run_back(): pl.pallas_call(back_kernel, grid=(inner // LANES,), in_specs=[columns_spe...  28.3 us
    ppermute x11, waiting for transfers between devices, chunk_permute(): return lax.ppermute(value, ('seq', 'head'), pairs)  20.4 us
    pallas_call x1, Pallas kernels, run_scan(): pl.pallas_call(scan_kernel, grid=(pairs,), in_specs=[columns_spec(length...  18.8 us
    dot_general x5, matrix products, dot_turned(): lax.dot_general(a, b, (((1,), (1,)), ((), ())), preferred_element_type=F32)  14.4 us
    unnamed x115, local copies, waits for them, and re-layouts  13.6 us
    pallas_call x1, Pallas kernels, run_gate(): pl.pallas_call(gate_kernel, grid=(length // tile,), in_specs=[rows_spec(t...  13.4 us
  transfers between devices with their start and end apart: 64, of which 25 were waited for; matrix products, arithmetic and copies ran while one was open for 33% of the time, Pallas kernels for 11%

profile of v1, /device:TPU:0, one launch (start us, length us, event | category | flops | bytes accessed | tf_op | source)
XLA Modules:
  0.0 410.7 jit_solution(8251539285065003655)
XLA Ops:
  35.2 7.6 %collective-permute-done.2 = bf16[2,96,384]{2,1,0:T(8,128)(2,1)S(1)} collective-permute-done((bf16[2,96,384]{2,1,0:T(8,128)(2,1)S(1)}, bf16[2,96,384]{2,1,0:T(8,128)(2,1)S(1)}, u32[]{:S(2)}, u32[]{:S(2)}) %collective-permute-start.2) | collective-permute-done | bytes 147488 | tf_op jit(solution)/shard_map/ppermute | solution.py:26
  46.2 5.6 %collective-permute-done.3 = bf16[4,96,384]{2,1,0:T(8,128)(2,1)S(1)} collective-permute-done((bf16[4,96,384]{2,1,0:T(8,128)(2,1)S(1)}, bf16[4,96,384]{2,1,0:T(8,128)(2,1)S(1)}, u32[]{:S(2)}, u32[]{:S(2)}) %collective-permute-start.3) | collective-permute-done | bytes 294944 | tf_op jit(solution)/shard_map/ppermute | solution.py:26
  57.3 7.1 %collective-permute-done.16 = bf16[2,48,768]{2,1,0:T(8,128)(2,1)S(1)} collective-permute-done((bf16[2,48,768]{2,1,0:T(8,128)(2,1)S(1)}, bf16[2,48,768]{2,1,0:T(8,128)(2,1)S(1)}, u32[]{:S(2)}, u32[]{:S(2)}) %collective-permute-start.16) | collective-permute-done | bytes 147488 | tf_op jit(solution)/shard_map/ppermute | solution.py:26
  67.8 4.1 %collective-permute-done.17 = bf16[4,48,768]{2,1,0:T(8,128)(2,1)S(1)} collective-permute-done((bf16[4,48,768]{2,1,0:T(8,128)(2,1)S(1)}, bf16[4,48,768]{2,1,0:T(8,128)(2,1)S(1)}, u32[]{:S(2)}, u32[]{:S(2)}) %collective-permute-start.17) | collective-permute-done | bytes 294944 | tf_op jit(solution)/shard_map/ppermute | solution.py:26
  82.2 3.8 collective-permute-done.18
  93.6 18.8 %scan_forward.1 = (bf16[512,1536]{1,0:T(8,128)(2,1)}, f32[512,1536]{1,0:T(8,128)}, f32[1536,128]{1,0:T(8,128)}, f32[512,1536]{1,0:T(8,128)}, f32[512,1536]{1,0:T...) custom-call(bf16[528,1536]{1,0:T(8,128)(2,1)} %convolution_convert_fusion.3.mixed_ref, ...), custom_call_target="tpu_custom_call" | custom-call | tf_op jit(solution)/shard_map/scan_forward/pallas_call | solution.py:486
  127.3 3.8 collective-permute-done.23
  141.0 3.6 collective-permute-done.24
  145.8 13.4 %gate_both.1 = (f32[512,1536]{1,0:T(8,128)}, bf16[512,1536]{1,0:T(8,128)(2,1)}, bf16[512,768]{1,0:T(8,128)(2,1)}, bf16[512,1536]{1,0:T(8,128)(2,1)}, bf16[512,15...) custom-call(f32[512,1536]{1,0:T(8,128)} %get-tuple-element.38.open_ref, ...), custom_call_target="tpu_custom_call" | custom-call | tf_op jit(solution)/shard_map/gate_both/pallas_call | solution.py:536
  168.1 5.2 %reshape.320 = bf16[8,96,4,384]{3,2,1,0:T(4,128)(2,1)} reshape(bf16[768,1536]{1,0:T(8,128)(2,1)} %convolution_convert_fusion.2) | data formatting | bytes 4718592 | tf_op jit(solution)/shard_map/reshape | solution.py:661
  180.6 4.4 %fusion.69 = f32[512,768]{1,0:T(8,128)} fusion(bf16[512,1536]{1,0:T(8,128)(2,1)S(1)} %copy-done.51, bf16[768,1536]{1,0:T(8,128)(2,1)} %bitcast.230), kind=kOutput, calls=%fused_computation.221 | convolution fusion | flops 1207959552 | bytes 5505024 | tf_op jit(solution)/shard_map/dot_general | solution.py:650
  185.0 6.8 %collective-permute-done.26 = bf16[1536,128]{1,0:T(8,128)(2,1)S(1)} collective-permute-done((bf16[1536,128]{1,0:T(8,128)(2,1)S(1)}, bf16[1536,128]{1,0:T(8,128)(2,1)S(1)}, u32[]{:S(2)}, u32[]{:S(2)}) %collective-permute-start.26) | collective-permute-done | bytes 393248 | tf_op jit(solution)/shard_map/ppermute | solution.py:106
  199.0 6.2 %collective-permute-done.27 = bf16[1536,128]{1,0:T(8,128)(2,1)S(1)} collective-permute-done((bf16[1536,128]{1,0:T(8,128)(2,1)S(1)}, bf16[1536,128]{1,0:T(8,128)(2,1)S(1)}, u32[]{:S(2)}, u32[]{:S(2)}) %collective-permute-start.27) | collective-permute-done | bytes 393248 | tf_op jit(solution)/shard_map/ppermute | solution.py:106
  206.7 28.3 %scan_backward.1 = (f32[528,1536]{1,0:T(8,128)}, f32[8,1536]{1,0:T(8,128)}, f32[528,256]{1,0:T(8,128)}, f32[8,256]{1,0:T(8,128)}, f32[512,128]{1,0:T(8,128)}, /*index=5*/f32[512,128]{1,0:T(8,128)}) custom-call(bf16[512,1536]{1,0:T(8,128)(2,1)} %get-tuple-element.39.x_ref, bf16[528,1536]{1,0:T(8,128)(2,1)} %convolution_convert_fusion.3.mixed_ref, ...), custom_call_target="tpu_custom_call" | custom-call | tf_op jit(solution)/shard_map/scan_backward/pallas_call | solution.py:584
  249.6 3.5 fusion.48
  255.2 5.9 %concatenate.240 = bf16[226376]{0:T(1024)(128)(2,1)S(1)} concatenate(bf16[196608]{0:T(1024)(128)(2,1)} %bitcast.240, bf16[18432]{0:T(1024)(128)(2,1)S(1)} %reshape.315, bf16[768]{0:T(1024)(128)(2,1)S(1)} %get-tuple-element.108, bf16[6144]{0:T(1024)(128)(2,1)S(1)} %reshape.316, bf16[1024]{0:T(1024)(128)(2,1)S(1)} %bitcast.265, bf16[1536]{0:T(1024)(128)(2,1)S(1)} %slice_reduce_fusion, ...), dimensions={0} | concatenate | bytes 905504 | tf_op jit(solution)/shard_map/concatenate | solution.py:878
  274.6 10.3 %collective-permute-done.31 = bf16[448,128]{1,0:T(8,128)(2,1)S(1)} collective-permute-done((bf16[448,128]{1,0:T(8,128)(2,1)S(1)}, bf16[448,128]{1,0:T(8,128)(2,1)S(1)}, u32[]{:S(2)}, u32[]{:S(2)}) %collective-permute-start.31) | collective-permute-done | bytes 114720 | tf_op jit(solution)/shard_map/ppermute | solution.py:26
  294.0 3.4 collective-permute-start.34
  309.9 3.4 collective-permute-done.56
  340.7 5.4 %collective-permute-done.41 = bf16[2,96,384]{2,1,0:T(8,128)(2,1)} collective-permute-done((bf16[2,96,384]{2,1,0:T(8,128)(2,1)S(1)}, bf16[2,96,384]{2,1,0:T(8,128)(2,1)}, u32[]{:S(2)}, u32[]{:S(2)}) %collective-permute-start.41) | collective-permute-done | bytes 147488 | tf_op jit(solution)/shard_map/ppermute | solution.py:26
  353.0 3.9 collective-permute-done.42
  364.7 12.4 %collective-permute-done.49 = bf16[2,96,384]{2,1,0:T(8,128)(2,1)S(1)} collective-permute-done((bf16[2,96,384]{2,1,0:T(8,128)(2,1)S(1)}, bf16[2,96,384]{2,1,0:T(8,128)(2,1)S(1)}, u32[]{:S(2)}, u32[]{:S(2)}) %collective-permute-start.49) | collective-permute-done | bytes 147488 | tf_op jit(solution)/shard_map/ppermute | solution.py:26
  377.4 5.3 %collective-permute-done.50 = bf16[1,96,384]{2,1,0:T(8,128)(2,1)S(1)} collective-permute-done((bf16[1,96,384]{2,1,0:T(8,128)(2,1)S(1)}, bf16[1,96,384]{2,1,0:T(8,128)(2,1)S(1)}, u32[]{:S(2)}, u32[]{:S(2)}) %collective-permute-start.50) | collective-permute-done | bytes 73760 | tf_op jit(solution)/shard_map/ppermute | solution.py:26
  395.3 6.4 %convert_add_fusion = f32[4,512,768]{2,1,0:T(8,128)} fusion(bf16[4,512,768]{2,1,0:T(8,128)(2,1)} %bitcast.226, bf16[4,512,768]{2,1,0:T(8,128)(2,1)} %param.33), kind=kLoop, calls=%fused_computation | loop fusion | flops 4718592 | bytes 12582912 | tf_op jit(solution)/shard_map/add | solution.py:858
  (416 shorter events, 215.0 us)
Async XLA Ops:
  7.2 388.1 %all-gather.5.cloned.1.call-start = ((), (), s32[]{:S(2)}) async-start(), calls=%async_computation | async-start | bytes 3932160 | tf_op jit(solution)/shard_map/all_gather | solution.py:803
  8.3 23.9 %collective-permute-start.1 = (bf16[1,96,384]{2,1,0:T(8,128)(2,1)S(1)}, bf16[1,96,384]{2,1,0:T(8,128)(2,1)S(1)}, u32[]{:S(2)}, u32[]{:S(2)}) collective-permute-start(bf16[1,96,384]{2,1,0:T(8,128)(2,1)S(1)} %dynamic-slice_bitcast_fusion.17), channel_id=1, source_target_pairs={{0,1},{1,0},{2,3},{3,2},{4,5},{5,4},{6,7},{7,6},{8,9},{9,8},{10,11... | collective-permute-start | bytes 221192 | tf_op jit(solution)/shard_map/ppermute | solution.py:26
  12.1 19.4 %collective-permute-start = (bf16[16,768]{1,0:T(8,128)(2,1)S(1)}, bf16[16,768]{1,0:T(8,128)(2,1)S(1)}, u32[]{:S(2)}, u32[]{:S(2)}) collective-permute-start(bf16[16,768]{1,0:T(8,128)(2,1)S(1)} %dynamic-slice_bitcast_fusion.19), channel_id=1, source_target_pairs={{0,4},{1,5},{2,6},{3,7},{4,8},{5,9},{6,10},{7,11},{8,12},{9,13},{1... | collective-permute-start | bytes 73736 | tf_op jit(solution)/shard_map/ppermute | solution.py:106
  18.1 36.3 %collective-permute-start.10 = (bf16[1,96,384]{2,1,0:T(8,128)(2,1)S(1)}, bf16[1,96,384]{2,1,0:T(8,128)(2,1)S(1)}, u32[]{:S(2)}, u32[]{:S(2)}) collective-permute-start(bf16[1,96,384]{2,1,0:T(8,128)(2,1)S(1)} %dynamic-slice_bitcast_fusion.16), channel_id=1, source_target_pairs={{0,1},{1,0},{2,3},{3,2},{4,5},{5,4},{6,7},{7,6},{8,9},{9,8},{10,11... | collective-permute-start | bytes 221192 | tf_op jit(solution)/shard_map/ppermute | solution.py:26
  27.0 26.4 %collective-permute-start.15 = (bf16[1,48,768]{2,1,0:T(8,128)(2,1)S(1)}, bf16[1,48,768]{2,1,0:T(8,128)(2,1)S(1)}, u32[]{:S(2)}, u32[]{:S(2)}) collective-permute-start(bf16[1,48,768]{2,1,0:T(8,128)(2,1)S(1)} %dynamic-slice_bitcast_fusion.15), channel_id=1, source_target_pairs={{0,1},{1,0},{2,3},{3,2},{4,5},{5,4},{6,7},{7,6},{8,9},{9,8},{10,11... | collective-permute-start | bytes 221192 | tf_op jit(solution)/shard_map/ppermute | solution.py:26
  28.8 17.4 %collective-permute-start.9 = (bf16[2,768,6]{1,2,0:T(8,128)(2,1)S(1)}, bf16[2,768,6]{1,2,0:T(8,128)(2,1)S(1)}, u32[]{:S(2)}, u32[]{:S(2)}) collective-permute-start(bf16[2,768,6]{1,2,0:T(8,128)(2,1)S(1)} %maximum_select_fusion.29), channel_id=1, source_target_pairs={{0,2},{1,3},{2,0},{3,1},{4,6},{5,7},{6,4},{7,5},{8,10},{9,11},{10,... | collective-permute-start | bytes 55304 | tf_op jit(solution)/shard_map/ppermute | solution.py:26
  31.5 21.9 %collective-permute-start.7 = (f32[2,2322]{1,0:T(2,128)S(1)}, f32[2,2322]{1,0:T(2,128)S(1)}, u32[]{:S(2)}, u32[]{:S(2)}) collective-permute-start(f32[2,2322]{1,0:T(2,128)S(1)} %maximum_select_fusion.30), channel_id=1, source_target_pairs={{0,2},{1,3},{2,0},{3,1},{4,6},{5,7},{6,4},{7,5},{8,10},{9,11},{10,... | collective-permute-start | bytes 55736 | tf_op jit(solution)/shard_map/ppermute | solution.py:26
  54.4 18.6 %collective-permute-start.11 = (bf16[2,96,384]{2,1,0:T(8,128)(2,1)S(1)}, bf16[2,96,384]{2,1,0:T(8,128)(2,1)S(1)}, u32[]{:S(2)}, u32[]{:S(2)}) collective-permute-start(bf16[2,96,384]{2,1,0:T(8,128)(2,1)S(1)} %maximum_select_fusion.21), channel_id=1, source_target_pairs={{0,2},{1,3},{2,0},{3,1},{4,6},{5,7},{6,4},{7,5},{8,10},{9,11},{10,... | collective-permute-start | bytes 442376 | tf_op jit(solution)/shard_map/ppermute | solution.py:26
  66.5 19.7 %collective-permute-start.5 = (bf16[16,96,384]{2,1,0:T(8,128)(2,1)S(1)}, bf16[16,96,384]{2,1,0:T(8,128)(2,1)}, u32[]{:S(2)}, u32[]{:S(2)}) collective-permute-start(bf16[16,96,384]{2,1,0:T(8,128)(2,1)S(1)} %maximum_select_fusion.3), channel_id=1, source_target_pairs={{0,4},{4,0},{8,12},{12,8},{16,20},{20,16},{24,28},{28,24},{1,5},{5... | collective-permute-start | bytes 3538952 | tf_op jit(solution)/shard_map/ppermute | solution.py:26
  79.3 37.1 %collective-permute-start.21 = (f32[1536]{0:T(1024)}, f32[1536]{0:T(1024)}, u32[]{:S(2)}, u32[]{:S(2)}) collective-permute-start(f32[1536]{0:T(1024)} %mul.234), channel_id=1, source_target_pairs={{0,8},{1,9},{2,10},{3,11},{4,12},{5,13},{6,14},{7,15},{8,0},{9,1},... | collective-permute-start | bytes 18440 | tf_op jit(solution)/shard_map/ppermute | solution.py:106
  81.1 36.0 %collective-permute-start.13 = (bf16[8,96,384]{2,1,0:T(8,128)(2,1)}, bf16[8,96,384]{2,1,0:T(8,128)(2,1)}, u32[]{:S(2)}, u32[]{:S(2)}) collective-permute-start(bf16[8,96,384]{2,1,0:T(8,128)(2,1)} %maximum_select_fusion.7), channel_id=1, source_target_pairs={{0,8},{4,12},{8,0},{12,4},{16,24},{20,28},{24,16},{28,20},{1,9},{5... | collective-permute-start | bytes 1769480 | tf_op jit(solution)/shard_map/ppermute | solution.py:26
  86.2 33.4 %collective-permute-start.19 = (bf16[16,48,768]{2,1,0:T(8,128)(2,1)S(1)}, bf16[16,48,768]{2,1,0:T(8,128)(2,1)}, u32[]{:S(2)}, u32[]{:S(2)}) collective-permute-start(bf16[16,48,768]{2,1,0:T(8,128)(2,1)S(1)} %maximum_select_fusion.5), channel_id=1, source_target_pairs={{0,4},{4,0},{8,12},{12,8},{16,20},{20,16},{24,28},{28,24},{1,5},{5... | collective-permute-start | bytes 3538952 | tf_op jit(solution)/shard_map/ppermute | solution.py:26
  119.0 16.7 %collective-permute-start.14 = (bf16[16,96,384]{2,1,0:T(8,128)(2,1)S(1)}, bf16[16,96,384]{2,1,0:T(8,128)(2,1)S(1)}, u32[]{:S(2)}, u32[]{:S(2)}) collective-permute-start(bf16[16,96,384]{2,1,0:T(8,128)(2,1)S(1)} %maximum_select_fusion.4), channel_id=1, source_target_pairs={{0,4},{4,0},{8,12},{12,8},{16,20},{20,16},{24,28},{28,24},{1,5},{5... | collective-permute-start | bytes 3538952 | tf_op jit(solution)/shard_map/ppermute | solution.py:26
  163.3 32.9 %collective-permute-start.54 = (bf16[16,48,768]{2,1,0:T(8,128)(2,1)}, bf16[16,48,768]{2,1,0:T(8,128)(2,1)}, u32[]{:S(2)}, u32[]{:S(2)}) collective-permute-start(bf16[16,48,768]{2,1,0:T(8,128)(2,1)} %dynamic-slice_bitcast_fusion), channel_id=1, source_target_pairs={{0,4},{4,0},{8,12},{12,8},{16,20},{20,16},{24,28},{28,24},{1,5},{5... | collective-permute-start | bytes 3538952 | tf_op jit(solution)/shard_map/ppermute | solution.py:26
  176.5 86.7 %collective-permute-start.38 = (bf16[16,96,384]{2,1,0:T(8,128)(2,1)}, bf16[16,96,384]{2,1,0:T(8,128)(2,1)}, u32[]{:S(2)}, u32[]{:S(2)}) collective-permute-start(bf16[16,96,384]{2,1,0:T(8,128)(2,1)} %dynamic-slice_bitcast_fusion.2), channel_id=1, source_target_pairs={{0,4},{4,0},{8,12},{12,8},{16,20},{20,16},{24,28},{28,24},{1,5},{5... | collective-permute-start | bytes 3538952 | tf_op jit(solution)/shard_map/ppermute | solution.py:26
  177.5 217.8 %all-gather.7.cloned.1.call-start = ((), (), s32[]{:S(2)}) async-start(), calls=%async_computation.1 | async-start | bytes 3932160 | tf_op jit(solution)/shard_map/all_gather | solution.py:857
  198.7 103.4 %collective-permute-start.55 = (bf16[8,48,768]{2,1,0:T(8,128)(2,1)}, bf16[8,48,768]{2,1,0:T(8,128)(2,1)}, u32[]{:S(2)}, u32[]{:S(2)}) collective-permute-start(bf16[8,48,768]{2,1,0:T(8,128)(2,1)} %dynamic-slice_bitcast_fusion.4), channel_id=1, source_target_pairs={{0,8},{4,12},{8,0},{12,4},{16,24},{20,28},{24,16},{28,20},{1,9},{5... | collective-permute-start | bytes 1769480 | tf_op jit(solution)/shard_map/ppermute | solution.py:26
  266.8 36.8 %collective-permute-start.39 = (bf16[8,96,384]{2,1,0:T(8,128)(2,1)}, bf16[8,96,384]{2,1,0:T(8,128)(2,1)}, u32[]{:S(2)}, u32[]{:S(2)}) collective-permute-start(bf16[8,96,384]{2,1,0:T(8,128)(2,1)} %dynamic-slice_bitcast_fusion.6), channel_id=1, source_target_pairs={{0,8},{4,12},{8,0},{12,4},{16,24},{20,28},{24,16},{28,20},{1,9},{5... | collective-permute-start | bytes 1769480 | tf_op jit(solution)/shard_map/ppermute | solution.py:26
  268.5 16.5 %collective-permute-start.31 = (bf16[448,128]{1,0:T(8,128)(2,1)S(1)}, bf16[448,128]{1,0:T(8,128)(2,1)S(1)}, u32[]{:S(2)}, u32[]{:S(2)}) collective-permute-start(bf16[448,128]{1,0:T(8,128)(2,1)S(1)} %dynamic-slice_bitcast_fusion.14), channel_id=1, source_target_pairs={{0,8},{4,12},{8,0},{12,4},{16,24},{20,28},{24,16},{28,20},{1,9},{5... | collective-permute-start | bytes 344072 | tf_op jit(solution)/shard_map/ppermute | solution.py:26
  287.9 48.4 %collective-permute-start.46 = (bf16[16,96,384]{2,1,0:T(8,128)(2,1)}, bf16[16,96,384]{2,1,0:T(8,128)(2,1)}, u32[]{:S(2)}, u32[]{:S(2)}) collective-permute-start(bf16[16,96,384]{2,1,0:T(8,128)(2,1)} %dynamic-slice_bitcast_fusion.1), channel_id=1, source_target_pairs={{0,4},{4,0},{8,12},{12,8},{16,20},{20,16},{24,28},{28,24},{1,5},{5... | collective-permute-start | bytes 3538952 | tf_op jit(solution)/shard_map/ppermute | solution.py:26
  313.5 21.9 %collective-permute-start.57 = (bf16[2,48,768]{2,1,0:T(8,128)(2,1)S(1)}, bf16[2,48,768]{2,1,0:T(8,128)(2,1)}, u32[]{:S(2)}, u32[]{:S(2)}) collective-permute-start(bf16[2,48,768]{2,1,0:T(8,128)(2,1)S(1)} %dynamic-slice_bitcast_fusion.11), channel_id=1, source_target_pairs={{0,2},{1,3},{2,0},{3,1},{4,6},{5,7},{6,4},{7,5},{8,10},{9,11},{10,... | collective-permute-start | bytes 442376 | tf_op jit(solution)/shard_map/ppermute | solution.py:26
  316.6 29.4 %collective-permute-start.41 = (bf16[2,96,384]{2,1,0:T(8,128)(2,1)S(1)}, bf16[2,96,384]{2,1,0:T(8,128)(2,1)}, u32[]{:S(2)}, u32[]{:S(2)}) collective-permute-start(bf16[2,96,384]{2,1,0:T(8,128)(2,1)S(1)} %dynamic-slice_bitcast_fusion.13), channel_id=1, source_target_pairs={{0,2},{1,3},{2,0},{3,1},{4,6},{5,7},{6,4},{7,5},{8,10},{9,11},{10,... | collective-permute-start | bytes 442376 | tf_op jit(solution)/shard_map/ppermute | solution.py:26
  359.7 17.3 %collective-permute-start.49 = (bf16[2,96,384]{2,1,0:T(8,128)(2,1)S(1)}, bf16[2,96,384]{2,1,0:T(8,128)(2,1)S(1)}, u32[]{:S(2)}, u32[]{:S(2)}) collective-permute-start(bf16[2,96,384]{2,1,0:T(8,128)(2,1)S(1)} %dynamic-slice_bitcast_fusion.12), channel_id=1, source_target_pairs={{0,2},{1,3},{2,0},{3,1},{4,6},{5,7},{6,4},{7,5},{8,10},{9,11},{10,... | collective-permute-start | bytes 442376 | tf_op jit(solution)/shard_map/ppermute | solution.py:26
  364.6 19.7 %collective-permute-start.61 = (bf16[4,48,768]{2,1,0:T(8,128)(2,1)S(1)}, bf16[4,48,768]{2,1,0:T(8,128)(2,1)S(1)}, u32[]{:S(2)}, u32[]{:S(2)}) collective-permute-start(bf16[4,48,768]{2,1,0:T(8,128)(2,1)S(1)} %maximum_select_fusion.18), channel_id=1, source_target_pairs={{0,4},{4,0},{8,12},{12,8},{16,20},{20,16},{24,28},{28,24},{1,5},{5... | collective-permute-start | bytes 884744 | tf_op jit(solution)/shard_map/ppermute | solution.py:26
  (92 other events, 884.5 us)
Sparse Core Ops, SparseCore 0:
  177.6 65.0 all-gather.4
  300.0 81.4 all-gather.6

commit v2 on v1

--- a/solution.py
+++ b/solution.py
@@ -1,3 +1,5 @@
+import functools
+
 import jax
 import jax.numpy as jnp
 from jax import lax
@@ -30,67 +32,92 @@
     return (lax.axis_index(axis) >> bit) & 1
 
 
-def joined(mine, other, upper):
+def joined(mine, other, upper, axis):
     return jnp.where(
         upper == 1,
-        jnp.concatenate([other, mine], axis=0),
-        jnp.concatenate([mine, other], axis=0),
-    )
-
-
-def seq_rank():
+        jnp.concatenate([other, mine], axis=axis),
+        jnp.concatenate([mine, other], axis=axis),
+    )
+
+
+def swap_orders():
     bits = bits_of(lax.axis_size("seq"))
-    return sum(bit_of("seq", b) << (bits - 1 - b) for b in range(bits))
-
-
-def gather_head(value):
-    for b in range(bits_of(lax.axis_size("head"))):
-        value = joined(value, swap(value, "head", b), bit_of("head", b))
-    return value
-
-
-def gather_seq(value):
-    for b in reversed(range(bits_of(lax.axis_size("seq")))):
-        value = joined(value, swap(value, "seq", b), bit_of("seq", b))
-    return value
-
-
-def gather_weight(weight):
-    seq_count, head_count = lax.axis_size("seq"), lax.axis_size("head")
-    part = weight.shape[0] // seq_count
-    own = lax.dynamic_slice_in_dim(weight, seq_rank() * part, part, 0)
-    whole = gather_seq(gather_head(own[None]))
-    return whole.reshape(seq_count, head_count, part, weight.shape[1])
-
-
-def halve(value, axis, bit):
-    value = value.reshape((2, value.shape[0] // 2) + value.shape[1:])
-    upper = bit_of(axis, bit)
-    keep = lax.dynamic_index_in_dim(value, upper, 0, keepdims=False)
-    send = lax.dynamic_index_in_dim(value, 1 - upper, 0, keepdims=False)
-    got = swap(send, axis, bit)
+    return list(range(1, bits)), list(reversed(range(1, bits)))
+
+
+def seq_rank(order):
+    return sum(bit_of("seq", b) << (len(order) - 1 - i) for i, b in enumerate(order))
+
+
+def join_seq(value, bit, axis):
+    return joined(value, swap(value, "seq", bit), bit_of("seq", bit), axis)
+
+
+def gather_blocks(value):
+    count, place = lax.axis_size("head"), lax.axis_index("head")
+    blocks = [value]
+    for d in range(1, count):
+        pairs = [(i, (i + d) % count) for i in range(count)]
+        blocks.insert(0, lax.ppermute(value, "head", pairs))
+    blocks = lax.dynamic_slice_in_dim(jnp.stack(blocks + blocks), count - 1 - place, count, 0)
+    return [blocks[h] for h in range(count)]
+
+
+def three_parts(value):
+    parts = []
+    for _ in range(3):
+        part = lax.reduce_precision(value, 8, 7)
+        parts.append(part.astype(BF16))
+        value = value - part
+    return parts
+
+
+def gather_columns(weight, extra):
+    first, second = swap_orders()
+    half, columns = weight.shape[0] // 2, weight.shape[1]
+    part = half // lax.axis_size("seq")
+    lines = -(-extra.shape[0] // (16 * columns)) * 16
+    extra_rows = jnp.pad(extra, (0, lines * columns - extra.shape[0])).reshape(lines, columns)
+    own = [
+        lax.dynamic_slice_in_dim(weight, at + seq_rank([0] + order) * part, part, 0)
+        for at, order in ((0, first), (half, second))
+    ]
+    blocks = gather_blocks(jnp.concatenate([*own, extra_rows], axis=0))
+    whole = jnp.concatenate([block[: 2 * part] for block in blocks], axis=1)
+    extras = jnp.stack([block[2 * part :].reshape(-1)[: extra.shape[0]] for block in blocks])
+    upper, lower = whole[:part], whole[part:]
+    for a, b in zip(reversed(first), reversed(second)):
+        upper, lower = join_seq(upper, a, 0), join_seq(lower, b, 0)
+    whole = join_seq(jnp.stack([upper, lower]), 0, 1)
+    return whole.reshape(weight.shape[0], whole.shape[2]), extras
+
+
+def halve(value, name, bit, axis):
+    size = value.shape[axis] // 2
+    upper = bit_of(name, bit)
+    keep = lax.dynamic_slice_in_dim(value, upper * size, size, axis)
+    send = lax.dynamic_slice_in_dim(value, (1 - upper) * size, size, axis)
+    got = swap(send, name, bit)
     return (keep.astype(F32) + got.astype(F32)).astype(value.dtype)
 
 
-def scatter_seq(value):
-    for b in range(bits_of(lax.axis_size("seq"))):
-        value = halve(value, "seq", b)
-    return value
-
-
-def reduce_weight(grad):
-    seq_count, head_count, part, width = grad.shape
-    grad = scatter_seq(grad.reshape(seq_count * head_count, part, width))
-    for b in reversed(range(bits_of(head_count))):
-        grad = halve(grad, "head", b)
-    return gather_seq(grad).reshape(seq_count * part, width)
-
-
-def reduce_all(value):
-    value = scatter_seq(value)
-    for b in range(bits_of(lax.axis_size("head"))):
-        value = (value.astype(F32) + swap(value, "head", b).astype(F32)).astype(value.dtype)
-    return gather_seq(value)
+def split_blocks(value, size):
+    count = value.shape[-1] // size
+    return jnp.stack([value[..., h * size : (h + 1) * size] for h in range(count)])
+
+
+def sum_blocks_step(blocks, shared, bit):
+    count = blocks.shape[0]
+    pairs = blocks.reshape((count // 2, 2) + blocks.shape[1:])
+    upper = bit_of("head", bit)
+    keep = lax.dynamic_index_in_dim(pairs, upper, 1, keepdims=False)
+    send = lax.dynamic_index_in_dim(pairs, 1 - upper, 1, keepdims=False)
+    shape = keep.shape
+    keep = jnp.concatenate([keep.reshape((-1,) + shape[2:]), shared], axis=0)
+    send = jnp.concatenate([send.reshape((-1,) + shape[2:]), shared], axis=0)
+    total = (keep.astype(F32) + swap(send, "head", bit).astype(F32)).astype(blocks.dtype)
+    most = shape[0] * shape[1]
+    return total[:most].reshape(shape), total[most:]
 
 
 def chunk_permute(value, rows, target):
@@ -106,22 +133,57 @@
     return lax.ppermute(value, ("seq", "head"), pairs)
 
 
-def carried(rate, state, rows, chunk, reverse):
+def carried(rate, state, rows, chunk, reverse, meanwhile):
     count = lax.axis_size("seq") * (lax.axis_size("head") // rows)
-    before = jnp.zeros_like(state)
+    levels = bits_of(count)
+    size = state.shape[0] // 2
+    heads = rate.shape[0]
+    side = chunk & 1
+    done = []
+
+    def exchange(value, rate, level, step):
+        coarse = lax.reduce_precision(rate, 8, 7)
+        fine = (rate - coarse).astype(BF16)
+        coarse = coarse.astype(BF16)
+        tail = jnp.pad(jnp.stack([coarse, fine]), ((0, 14), (0, STATE - heads)))
+        message = jnp.concatenate([value.astype(BF16), tail], axis=0)
+        got = chunk_permute(message, rows, lambda c: c ^ (1 << level))
+        got, extra = lax.optimization_barrier((got, meanwhile[step]() if step < len(meanwhile) else ()))
+        done.append(extra)
+        pair = got[size : size + 2, :heads].astype(F32)
+        return got[:size].astype(F32), pair[0] + pair[1]
+
+    def widen(rate):
+        return lax.dynamic_slice_in_dim(jnp.repeat(rate, HEADDIM), side * size, size, 0)[:, None]
+
+    low = state.astype(BF16)
+    send = lax.dynamic_slice_in_dim(low, (1 - side) * size, size, 0)
+    mine = lax.dynamic_slice_in_dim(state, side * size, size, 0)
+    theirs, their_rate = exchange(send, rate, 0, 0)
+    comes_second = side == (0 if reverse else 1)
+    earlier = jnp.where(comes_second, theirs, mine)
+    later = jnp.where(comes_second, mine, theirs)
+    first_rate = jnp.where(comes_second, their_rate, rate)
+    second_rate = jnp.where(comes_second, rate, their_rate)
+    total = widen(second_rate) * earlier + later
+    total_rate = rate * their_rate
+    before = jnp.zeros_like(total)
     before_rate = jnp.ones_like(rate)
-    for b in range(bits_of(count)):
-        got = chunk_permute(state.astype(BF16), rows, lambda c: c ^ (1 << b)).astype(F32)
-        got_rate = chunk_permute(rate, rows, lambda c: c ^ (1 << b))
+    for b in range(1, levels):
+        got, got_rate = exchange(total, total_rate, b, b)
         after = ((chunk >> b) & 1) == (0 if reverse else 1)
-        before = jnp.where(after, before_rate[:, None] * got + before, before)
+        before = jnp.where(after, widen(before_rate) * got + before, before)
         before_rate = jnp.where(after, before_rate * got_rate, before_rate)
-        if b < bits_of(count) - 1:
-            state = jnp.where(
-                after, rate[:, None] * got + state, got_rate[:, None] * state + got
+        if b < levels - 1:
+            total = jnp.where(
+                after, widen(total_rate) * got + total, widen(got_rate) * total + got
             )
-            rate = rate * got_rate
-    return before
+            total_rate = total_rate * got_rate
+    second = widen(first_rate) * before + earlier
+    own = jnp.where(comes_second, second, before).astype(BF16)
+    other = jnp.where(comes_second, before, second).astype(BF16)
+    got = chunk_permute(other, rows, lambda c: c ^ 1)
+    return joined(own, got, side, 0), done
 
 
 def contract(a, b, dims):
@@ -311,6 +373,10 @@
         grad_start_ref[...] += grad_start
 
 
+def first_pair(first, count):
+    return 0 if first else count
+
+
 def conv_back(grad_act, padded, kernel, bias, masks):
     length, width = grad_act.shape
     taps = taps_of(padded, masks)
@@ -333,41 +399,40 @@
     return mixed, sums
 
 
-def back_kernel(
-    x_ref,
-    mixed_ref,
-    run_ref,
-    size_ref,
-    grad_scan_ref,
-    total_ref,
-    grad_end_ref,
-    start_ref,
-    kernel_ref,
-    bias_ref,
-    skip_ref,
-    states_ref,
-    kernel_state_ref,
-    bias_state_ref,
-    masks_ref,
-    seg_col_ref,
-    seg_row_ref,
-    writers_ref,
-    readers_ref,
-    turned_ref,
-    grad_read_ref,
-    grad_mixed_ref,
-    sums_ref,
-    grad_states_ref,
-    sums_state_ref,
-    rate_ref,
-    direct_ref,
-    scores,
-    grad_scores,
-    grad_write,
-    rate_sum,
-    direct_sum,
-):
-    pair = pl.program_id(0)
+def back_kernel(first, last, *refs):
+    (
+        x_ref,
+        mixed_ref,
+        run_ref,
+        size_ref,
+        grad_scan_ref,
+        total_ref,
+        grad_end_ref,
+        start_ref,
+        kernel_ref,
+        bias_ref,
+        skip_ref,
+        masks_ref,
+        seg_col_ref,
+        seg_row_ref,
+        writers_ref,
+        readers_ref,
+        turned_ref,
+    ) = refs[:17]
+    refs = refs[17:]
+    if last:
+        states_ref, kernel_state_ref, bias_state_ref, grad_read_ref = refs[:4]
+        refs = refs[4:]
+    sums_in = () if first else refs[:4]
+    refs = refs[len(sums_in) :]
+    grad_mixed_ref, sums_ref = refs[:2]
+    refs = refs[2:]
+    scores, grad_scores, grad_write, rate_sum, direct_sum = refs[-5:]
+    refs = refs[:-5]
+    if last:
+        grad_states_ref, sums_state_ref, rate_ref, direct_ref = refs
+    place = pl.program_id(0)
+    pair = place + first_pair(first, pl.num_programs(0))
     length = x_ref.shape[0]
     low = lax.broadcasted_iota(jnp.int32, (1, LANES), 1) < HEADDIM
     lane = lax.broadcasted_iota(jnp.int32, (1, LANES), 1)
@@ -376,14 +441,14 @@
     readers = readers_ref[...]
     seg_col = seg_col_ref[...]
 
-    @pl.when(pair == 0)
+    totals = (grad_scores, grad_write, rate_sum, direct_sum)
+
+    @pl.when(place == 0)
     def _():
         linked = linked_of(seg_col, seg_row_ref[...])
         scores[...] = contract(readers, writers, ((1,), (1,))) * linked
-        grad_scores[...] = jnp.zeros_like(grad_scores)
-        grad_write[...] = jnp.zeros_like(grad_write)
-        rate_sum[...] = jnp.zeros_like(rate_sum)
-        direct_sum[...] = jnp.zeros_like(direct_sum)
+        for i, total in enumerate(totals):
+            total[...] = jnp.zeros_like(total) if first else sums_in[i][...]
 
     run = run_ref[...]
     size = size_ref[...]
@@ -408,8 +473,8 @@
             inner[s] = part if inner[s] is None else inner[s] + part
         grad_scores[cut(t), cut(s)] = grad_score
     inner = inner[0] if len(inner) == 1 else jnp.concatenate(inner, axis=0)
-    last = jnp.where(seg_col == seg_col[length - 1 : length, :], 1.0, 0.0)
-    toward = last * jnp.exp(run[length - 1 : length, :] - run)
+    final = jnp.where(seg_col == seg_col[length - 1 : length, :], 1.0, 0.0)
+    toward = final * jnp.exp(run[length - 1 : length, :] - run)
     grad_end = grad_end_ref[...]
     outer = toward * contract(writers, grad_end.astype(BF16), ((1,), (1,)))
     grad_write[...] += contract(
@@ -441,8 +506,12 @@
     sums = jnp.where(rows == 6, kept_low, jnp.where(rows == 7, kept_high, sums))
     sums_ref[...] = sums
 
-    @pl.when(pair == pl.num_programs(0) - 1)
+    @pl.when(place == pl.num_programs(0) - 1)
     def _():
+        if not last:
+            for ref, total in zip(refs, totals):
+                ref[...] = total[...]
+            return
         linked = linked_of(seg_col, seg_row_ref[...])
         grad_score = (grad_scores[...] * linked).astype(BF16)
         grad_readers = contract(grad_score, writers, ((1,), (0,))) + grad_read_ref[...]
@@ -575,67 +644,40 @@
     )(opened, x, run, gate, grad_out, hidden, entered, readers, start, weight, gain, skip)
 
 
-def run_back(
-    x, mixed, run, size, grad_scan, total, grad_end, start, kernel, bias, skip,
-    states, kernel_state, bias_state, masks, seg_col, seg_row, writers, readers, turned, grad_read,
-):
+def run_back(first, wide_args, rows_args, row_args, whole_args, last_args, sums_in):
+    x = wide_args[0]
     length, inner = x.shape
     wide = 2 * STATE
+    pairs = inner // LANES
+    at = 0
+    last = True
+
+    def columns(rows, offset):
+        return pl.BlockSpec((rows, LANES), lambda i: (0, i + offset))
+
+    args = [*wide_args, *rows_args, *row_args, *whole_args, *last_args, *sums_in]
+    in_specs = (
+        [columns(a.shape[0], at) for a in wide_args]
+        + [pl.BlockSpec((LANES, STATE), lambda i: (i + at, 0)) for a in rows_args]
+        + [columns(a.shape[0], at) for a in row_args]
+        + [whole_spec(a.shape) for a in (*whole_args, *last_args, *sums_in)]
+    )
+    sum_shapes = [(length, length), (length, STATE), (length, LANES), (length, LANES)]
+    out_shapes = [(length + HALO, inner), (8, inner)]
+    out_specs = [columns(length + HALO, 0), columns(8, 0)]
+    more = [(length + HALO, wide), (8, wide), (length, LANES), (length, LANES)] if last else sum_shapes
+    out_specs += [whole_spec(shape) for shape in more]
     return pl.pallas_call(
-        back_kernel,
-        grid=(inner // LANES,),
-        in_specs=[
-            columns_spec(length),
-            columns_spec(length + HALO),
-            columns_spec(length),
-            columns_spec(length),
-            columns_spec(length),
-            columns_spec(length),
-            rows_spec(LANES, STATE),
-            rows_spec(LANES, STATE),
-            columns_spec(4),
-            columns_spec(1),
-            columns_spec(1),
-            whole_spec((length + HALO, wide)),
-            whole_spec((4, wide)),
-            whole_spec((1, wide)),
-            whole_spec((length, 4)),
-            whole_spec((length, 1)),
-            whole_spec((1, length)),
-            whole_spec((length, STATE)),
-            whole_spec((length, STATE)),
-            whole_spec((LANES, length)),
-            whole_spec((length, STATE)),
-        ],
-        out_specs=[
-            columns_spec(length + HALO),
-            columns_spec(8),
-            whole_spec((length + HALO, wide)),
-            whole_spec((8, wide)),
-            whole_spec((length, LANES)),
-            whole_spec((length, LANES)),
-        ],
-        out_shape=[
-            jax.ShapeDtypeStruct((length + HALO, inner), F32),
-            jax.ShapeDtypeStruct((8, inner), F32),
-            jax.ShapeDtypeStruct((length + HALO, wide), F32),
-            jax.ShapeDtypeStruct((8, wide), F32),
-            jax.ShapeDtypeStruct((length, LANES), F32),
-            jax.ShapeDtypeStruct((length, LANES), F32),
-        ],
-        scratch_shapes=[
-            pltpu.VMEM((length, length), F32),
-            pltpu.VMEM((length, length), F32),
-            pltpu.VMEM((length, STATE), F32),
-            pltpu.VMEM((length, LANES), F32),
-            pltpu.VMEM((length, LANES), F32),
-        ],
+        functools.partial(back_kernel, first, last),
+        grid=(pairs,),
+        in_specs=in_specs,
+        out_specs=out_specs,
+        out_shape=[jax.ShapeDtypeStruct(shape, F32) for shape in out_shapes + more],
+        scratch_shapes=[pltpu.VMEM((length, length), F32)]
+        + [pltpu.VMEM(shape, F32) for shape in sum_shapes],
         compiler_params=pltpu.CompilerParams(vmem_limit_bytes=VMEM_LIMIT),
         name="scan_backward",
-    )(
-        x, mixed, run, size, grad_scan, total, grad_end, start, kernel, bias, skip,
-        states, kernel_state, bias_state, masks, seg_col, seg_row, writers, readers, turned, grad_read,
-    )
+    )(*args)
 
 
 def dot(a, b):
@@ -648,34 +690,6 @@
 
 def dot_turned(a, b):
     return lax.dot_general(a, b, (((1,), (1,)), ((), ())), preferred_element_type=F32)
-
-
-def to_columns(gathered):
-    seq_count, head_count, part, width = gathered.shape
-    return gathered.transpose(0, 2, 1, 3).reshape(seq_count * part, head_count * width)
-
-
-def from_columns(grad, head_count):
-    seq_count = lax.axis_size("seq")
-    rows, columns = grad.shape
-    split = grad.astype(BF16).reshape(
-        seq_count, rows // seq_count, head_count, columns // head_count
-    )
-    return split.transpose(0, 2, 1, 3)
-
-
-def to_rows(gathered):
-    seq_count, head_count, part, width = gathered.shape
-    return gathered.transpose(1, 0, 2, 3).reshape(seq_count * head_count * part, width)
-
-
-def from_rows(grad, head_count):
-    seq_count = lax.axis_size("seq")
-    rows, columns = grad.shape
-    split = grad.astype(BF16).reshape(
-        head_count, seq_count, rows // (seq_count * head_count), columns
-    )
-    return split.transpose(1, 0, 2, 3)
 
 
 def pad_lanes(value):
@@ -714,15 +728,30 @@
     heads = local_heads * head_devices
     taps = kernel_value.shape[0]
 
-    value_full = to_columns(gather_weight(value_weight))
-    gate_full = to_columns(gather_weight(gate_weight))
-    output_full = to_rows(gather_weight(output_weight))
-    step_full = gather_head(step_weight[None])
-    step_full = step_full.transpose(1, 0, 2).reshape(width, heads)
     small = jnp.concatenate(
         [kernel_value.reshape(-1), bias_value, inner_gain, step_bias, decay_log, skip_gain]
     )
-    small = gather_head(small[None])
+    count = small.shape[0]
+    value_full, extras = gather_columns(
+        value_weight, jnp.concatenate([*three_parts(small), step_weight.reshape(-1)])
+    )
+    small = sum(extras[:, i * count : (i + 1) * count].astype(F32) for i in range(3))
+    step_full = extras[:, 3 * count :].reshape(head_devices, width, local_heads)
+    step_full = step_full.transpose(1, 0, 2).reshape(width, heads)
+    seq_count = lax.axis_size("seq")
+    part = width // seq_count
+    out_part = local_inner // seq_count
+    packed = jnp.concatenate(
+        [
+            lax.dynamic_slice_in_dim(gate_weight, seq_index * part, part, 0),
+            lax.dynamic_slice_in_dim(output_weight, seq_index * out_part, out_part, 0).reshape(
+                part, local_inner
+            ),
+        ],
+        axis=0,
+    )
+    packed = lax.all_gather(packed, ("seq", "head"))
+    packed = packed.reshape(seq_count, head_devices, 2 * part, local_inner)
     at = taps * local_inner
     kernel_full = small[:, :at].reshape(head_devices, taps, local_inner)
     kernel_full = kernel_full.transpose(1, 0, 2).reshape(taps, inner)
@@ -766,7 +795,6 @@
     step_size = jax.nn.softplus(step_raw)
     log_decay = -step_size * decay_full
     passing = jnp.exp(jnp.sum(log_decay, axis=0)) * (segments[length - 1] == before).astype(F32)
-    passing_wide = jnp.repeat(passing, HEADDIM)
 
     kernel_rows = kernel_full
     bias_state_row = bias_state[None]
@@ -783,9 +811,20 @@
         pad_lanes(step_size),
         pad_lanes(log_decay),
     )
-    start = carried(passing_wide, end_state, rows, chunk, False).astype(BF16)
-    gate_pre = dot(normed, gate_full)
-    grad_out_in = dot_turned(cot, output_full)
+    def make_gate():
+        gate_full = packed[:, :, :part].transpose(0, 2, 1, 3).reshape(width, inner)
+        return gate_full, dot(normed, gate_full)
+
+    def make_out():
+        output_full = packed[:, :, part:].reshape(seq_count, head_devices, out_part, width)
+        output_full = output_full.transpose(1, 0, 2, 3).reshape(inner, width)
+        return output_full, dot_turned(cot, output_full)
+
+    start, done = carried(
+        passing, end_state, rows, chunk, False, (tuple, make_gate, make_out)
+    )
+    gate_full, gate_pre = done[1]
+    output_full, grad_out_in = done[2]
     total, out_in, block_rows, grad_scan, grad_gate, grad_read, gate_sums, grad_start = run_gate(
         opened,
         x,
@@ -801,37 +840,44 @@
         skip_wide,
     )
     block_output = lax.all_gather(block_rows, "head").reshape(rows, block, width)
-    grad_output_weight = reduce_weight(from_rows(dot_rows(out_in, cot), head_devices))
-    grad_gate_weight = reduce_weight(from_columns(dot_rows(normed, grad_gate), head_devices))
-    grad_end = carried(passing_wide, grad_start, rows, chunk, True)
-    grad_mixed, sums, grad_states, state_sums, rate, direct = run_back(
-        x,
-        mixed,
-        run,
-        size,
-        grad_scan,
-        total,
-        grad_end,
-        start,
-        kernel_rows,
-        bias_full,
-        skip_wide,
-        states,
-        kernel_state,
-        bias_state_row,
-        masks,
-        seg_col,
-        seg_row,
-        writers,
-        readers,
-        turned,
-        grad_read,
-    )
-    edge_values = chunk_permute(grad_mixed[HALO - 8 : HALO], rows, lambda c: c - 1)
-    edge_states = chunk_permute(grad_states[HALO - 8 : HALO], rows, lambda c: c - 1)
+    first, second = swap_orders()
+
+    def early_start():
+        return (
+            halve(dot_rows(cot, out_in).astype(BF16), "seq", 0, 0),
+            halve(dot_rows(normed, grad_gate).astype(BF16), "seq", 0, 0),
+            dot_turned(grad_gate, gate_full),
+        )
+
+    grad_end, done = carried(passing, grad_start, rows, chunk, True, (tuple, early_start))
+    out_grad, gate_grad, grad_normed = done[1]
+    out_grad, gate_grad, grad_end = lax.optimization_barrier((out_grad, gate_grad, grad_end))
+    out_grad = halve(out_grad, "seq", first[0], 0)
+    gate_grad = halve(gate_grad, "seq", second[0], 0)
+    groups = (
+        (x, mixed, run, size, grad_scan, total),
+        (grad_end, start),
+        (kernel_rows, bias_full, skip_wide),
+        (masks, seg_col, seg_row, writers, readers, turned),
+    )
+    last_args = (states, kernel_state, bias_state_row, grad_read)
+    back = run_back(True, *groups, last_args, ())
+    back, out_grad, gate_grad = lax.optimization_barrier((back, out_grad, gate_grad))
+    grad_mixed, sums, grad_states, state_sums, rate, direct = back
+    for a, b in zip(first[1:], second[1:]):
+        out_grad = halve(out_grad, "seq", a, 0)
+        gate_grad = halve(gate_grad, "seq", b, 0)
+    edges = jnp.concatenate([grad_mixed[HALO - 8 : HALO], grad_states[HALO - 8 : HALO]], axis=1)
+    edges = chunk_permute(edges, rows, lambda c: c - 1)
+    edges, out_grad, gate_grad = lax.optimization_barrier((edges, out_grad, gate_grad))
+    early = split_blocks(jnp.stack([out_grad, gate_grad]), local_inner)
+    none = early[0][:0]
+    for b in range(bits_of(head_devices)):
+        early, none = sum_blocks_step(early, none, b)
+    early = early[0]
     fill = ((length - 8, 0), (0, 0))
-    grad_values_in = (grad_mixed[HALO:] + jnp.pad(edge_values, fill)).astype(BF16)
-    grad_states_in = (grad_states[HALO:] + jnp.pad(edge_states, fill)).astype(BF16)
+    grad_values_in = (grad_mixed[HALO:] + jnp.pad(edges[:, :inner], fill)).astype(BF16)
+    grad_states_in = (grad_states[HALO:] + jnp.pad(edges[:, inner:], fill)).astype(BF16)
 
     kept = jnp.stack([sums[6].reshape(-1, LANES).sum(1), sums[7].reshape(-1, LANES).sum(1)], axis=1)
     rate_end = sums[5].reshape(heads, HEADDIM).sum(1) + passing * kept.reshape(heads)
@@ -844,7 +890,7 @@
     grad_skip_gain = gate_sums[1].reshape(heads, HEADDIM).sum(1)
 
     grad_normed = (
-        dot_turned(grad_gate, gate_full)
+        grad_normed
         + dot_turned(grad_values_in, value_full)
         + dot_turned(grad_states_in, state_weight)
         + dot_turned(grad_step_in, step_full)
@@ -854,17 +900,11 @@
     change = norm_scale * grad_unit - hidden * norm_scale**3 * jnp.mean(
         grad_unit * hidden, axis=1, keepdims=True
     )
-    changes = lax.all_gather(change.astype(BF16), "head").reshape(rows, block, width)
+    change, early = lax.optimization_barrier((change.astype(BF16), early))
+    changes = lax.all_gather(change, "head").reshape(rows, block, width)
     input_gradient = cotangent.astype(F32) + changes.astype(F32)
 
-    grad_value_weight = reduce_weight(
-        from_columns(dot_rows(normed, grad_values_in), head_devices)
-    )
-    grad_state_weight = dot_rows(normed, grad_states_in)
-    grad_step_weight = dot_rows(normed, grad_step_in)
     pieces = [
-        grad_state_weight,
-        grad_step_weight,
         grad_norm_gain,
         sums[:taps],
         state_sums[:taps],
@@ -875,15 +915,59 @@
         grad_skip_gain,
         gate_sums[0],
     ]
-    flat = jnp.concatenate([piece.reshape(-1) for piece in pieces]).astype(BF16)
-    unit = lax.axis_size("seq") * 16 * LANES
-    padded = -(-flat.shape[0] // unit) * unit
-    flat = jnp.pad(flat, (0, padded - flat.shape[0])).reshape(-1, LANES)
-    flat = reduce_all(flat).reshape(-1).astype(F32)
+    flat = jnp.concatenate([piece.reshape(-1) for piece in pieces])
+    lines = -(-flat.shape[0] // (8 * LANES)) * 8
+    flat = jnp.pad(flat, (0, lines * LANES - flat.shape[0])).reshape(lines, LANES)
+    tail = jnp.concatenate(
+        [
+            dot_rows(normed, grad_values_in).astype(BF16),
+            dot_rows(normed, grad_states_in).astype(BF16),
+            dot_rows(normed, pad_lanes(grad_step_in)).astype(BF16),
+        ],
+        axis=1,
+    )
+    tail = tail.reshape(2, width // 2, tail.shape[1])
+
+    tail = halve(tail, "seq", 0, 1)
+    flat = flat + swap(flat, "seq", 0)
+    upper, lower = tail[0], tail[1]
+    for a, b in zip(first, second):
+        upper, lower = halve(upper, "seq", a, 0), halve(lower, "seq", b, 0)
+        flat = flat + swap(flat, "seq", a)
+    tail = jnp.stack([upper, lower])
+    part = tail.shape[1]
+    blocks = split_blocks(tail[:, :, :inner], local_inner)
+    shared = split_blocks(tail[:, :, inner:], local_inner)
+    wide = shared.shape[0]
+    shared = shared.reshape((-1,) + shared.shape[2:])
+    for b in range(bits_of(head_devices)):
+        blocks, shared = sum_blocks_step(blocks, shared, b)
+        flat = flat + swap(flat, "head", b)
+    blocks = blocks[0]
+    late = (1 + wide) * local_inner
+    sides = []
+    for i in range(2):
+        own_part = jnp.concatenate([blocks[i], *shared[i::2]], axis=1)
+        other = jnp.concatenate([early[i, :part], early[i, part:]], axis=1)
+        other = jnp.pad(other, ((0, 0), (0, late - other.shape[1])))
+        sides.append(jnp.concatenate([own_part, other], axis=0)[None])
+    upper, lower = sides
+    for a, b in zip(reversed(first), reversed(second)):
+        upper, lower = join_seq(upper, a, 0), join_seq(lower, b, 0)
+    sides = join_seq(jnp.stack([upper, lower], axis=1), 0, 0).astype(F32)
+    tail = sides[:, :, :part].transpose(1, 0, 2, 3).reshape(width, late)
+    early = sides[:, :, part:, : 2 * local_inner].reshape(seq_count, 2, part, 2, local_inner)
+    early = early.transpose(1, 0, 3, 2, 4).reshape(2, width, local_inner)
+    grad_output_weight = early[0].T
+    grad_gate_weight = early[1]
+    grad_value_weight = tail[:, :local_inner]
+    shared = tail[:, local_inner:]
+    flat = flat.reshape(-1)
     summed, at = [], 0
     for piece in pieces:
         summed.append(flat[at : at + piece.size].reshape(piece.shape))
         at += piece.size
+    summed = [shared[:, : 2 * STATE], shared[:, 2 * STATE : 2 * STATE + heads]] + summed
 
     def own(value, axis):
         size = value.shape[axis] // head_devices
@@ -893,8 +977,8 @@
         block_output,
         input_gradient,
         summed[2],
-        grad_gate_weight.astype(F32),
-        grad_value_weight.astype(F32),
+        grad_gate_weight,
+        grad_value_weight,
         summed[0],
         own(summed[1], 1),
         own(summed[3], 1),
@@ -905,7 +989,7 @@
         own(summed[8], 0),
         own(summed[9], 0),
         own(summed[10], 0),
-        grad_output_weight.astype(F32),
+        grad_output_weight,
     )
 
 

time: 417 us -> 356 us (0.85)
  waiting for transfers between devices: 107 us -> 80.4 us
  starting transfers between devices: 69.1 us -> 47 us
  other arithmetic: 51.4 us -> 44.6 us
  matrix products: 32.6 us -> 27.6 us
    ppermute x51 -> x30, starting transfers between devices: 59.2 us -> 33.5 us  [swap(): return lax.ppermute(value, axis, [(i, i ^ 1 << bit) for i in range(count)])]
    ppermute x51 -> x30, waiting for transfers between devices: 86.8 us -> 68.4 us  [swap(): return lax.ppermute(value, axis, [(i, i ^ 1 << bit) for i in range(count)])]
    ppermute x11 -> x10, waiting for transfers between devices: 20.4 us -> 9.55 us  [chunk_permute(): return lax.ppermute(value, ('seq', 'head'), pairs)]
    slice x4 -> x17, local copies, waits for them, and re-layouts: 3.03 us -> 10.7 us  [the longest x1 3.02 us: make_out(): packed[:, :, part:].reshape(seq_count, head_devices, out_part, width)]
    dynamic_slice x0 -> x26, local copies, waits for them, and re-layouts: none -> 7.54 us  [the longest x11 4.15 us: halve(): send = lax.dynamic_slice_in_dim(value, (1 - upper) * size, size, axis)]
    select_n x30 -> x13, other arithmetic: 10.5 us -> 4.33 us  [the longest x11 4.31 us: joined(): jnp.where(upper == 1, jnp.concatenate([other, mine], axis=axis), jnp.conc...]
    ppermute x0 -> x3, starting transfers between devices: none -> 6.11 us  [gather_blocks(): blocks.insert(0, lax.ppermute(value, 'head', pairs))]
    convert_element_type x14 -> x26, other arithmetic: 18 us -> 12.3 us  [the longest x4 4.19 us: exchange(): message = jnp.concatenate([value.astype(BF16), tail], axis=0)]
  transfers between devices with their start and end apart: 64 -> 46, of which waited for: 25 -> 22; matrix products, arithmetic and copies ran while one was open for 33% -> 32% of each run, Pallas kernels for 11% -> 14%
where the time goes in v2:
time: 356 us; the launch traced here: 349 us
  waiting for transfers between devices  80.4 us (23%)
  local copies, waits for them, and re-layouts  72 us (20%)
  Pallas kernels  60.9 us (17%)
  starting transfers between devices  47 us (13%)
  other arithmetic  44.6 us (13%)
  matrix products  27.6 us (8%)
  between operations  16.7 us (5%)
    ppermute x30, waiting for transfers between devices, swap(): return lax.ppermute(value, axis, [(i, i ^ 1 << bit) for i in range(count)])  68.4 us
    ppermute x30, starting transfers between devices, swap(): return lax.ppermute(value, axis, [(i, i ^ 1 << bit) for i in range(count)])  33.5 us
    pallas_call x1, Pallas kernels, run_back(): pl.pallas_call(functools.partial(back_kernel, first, last), grid=(pairs,)...  28.5 us
    pallas_call x1, Pallas kernels, run_scan(): pl.pallas_call(scan_kernel, grid=(pairs,), in_specs=[columns_spec(length...  18.9 us
    unnamed x109, local copies, waits for them, and re-layouts  14.3 us
    pallas_call x1, Pallas kernels, run_gate(): pl.pallas_call(gate_kernel, grid=(length // tile,), in_specs=[rows_spec(t...  13.4 us
    dot_general x5, matrix products, dot_turned(): lax.dot_general(a, b, (((1,), (1,)), ((), ())), preferred_element_type=F32)  11.3 us
    ppermute x10, waiting for transfers between devices, chunk_permute(): return lax.ppermute(value, ('seq', 'head'), pairs)  9.55 us
  transfers between devices with their start and end apart: 46, of which 22 were waited for; matrix products, arithmetic and copies ran while one was open for 32% of the time, Pallas kernels for 14%

profile of v2, /device:TPU:0, one launch (start us, length us, event | category | flops | bytes accessed | tf_op | source)
XLA Modules:
  0.0 349.3 jit_solution(1595673755113080979)
XLA Ops:
  11.0 5.1 %collective-permute-start.1 = (bf16[128,384]{1,0:T(8,128)(2,1)S(1)}, bf16[128,384]{1,0:T(8,128)(2,1)S(1)}, u32[]{:S(2)}, u32[]{:S(2)}) collective-permute-start(bf16[128,384]{1,0:T(8,128)(2,1)S(1)} %pad_maximum_fusion.19), channel_id=1, source_target_pairs={{0,3},{1,0},{2,1},{3,2},{4,7},{5,4},{6,5},{7,6},{8,11},{9,8},{10,9... | collective-permute-start | bytes 294920 | tf_op jit(solution)/shard_map/ppermute | solution.py:61
  44.3 3.8 %collective-permute-done.5 = bf16[96,1536]{1,0:T(8,128)(2,1)S(1)} collective-permute-done((bf16[96,1536]{1,0:T(8,128)(2,1)S(1)}, bf16[96,1536]{1,0:T(8,128)(2,1)S(1)}, u32[]{:S(2)}, u32[]{:S(2)}) %collective-permute-start.5) | collective-permute-done | bytes 294944 | tf_op jit(solution)/shard_map/ppermute | solution.py:28
  59.0 18.9 %scan_forward.1 = (bf16[512,1536]{1,0:T(8,128)(2,1)}, f32[512,1536]{1,0:T(8,128)}, f32[1536,128]{1,0:T(8,128)}, f32[512,1536]{1,0:T(8,128)}, f32[512,1536]{1,0:T...) custom-call(bf16[528,1536]{1,0:T(8,128)(2,1)} %convolution_convert_fusion.3.mixed_ref.refs_1_, ...), custom_call_target="tpu_custom_call" | custom-call | tf_op jit(solution)/shard_map/scan_forward/pallas_call | solution.py:555
  86.0 3.0 fusion.100
  91.4 3.1 fusion.30.gate_ref
  103.5 4.8 %fusion.11.grad_out_ref = f32[512,1536]{1,0:T(8,128)} fusion(bf16[1536,768]{1,0:T(8,128)(2,1)S(1)} %bitcast.230, bf16[4,512,768]{2,1,0:T(8,128)(2,1)} %param.33, s32[]{:T(128)S(6)} %select_n.395), kind=kOutput, calls=%fused_computation.39 | convolution fusion | flops 1207959552 | bytes 6291460 | tf_op jit(solution)/shard_map/dot_general | solution.py:692
  112.2 13.4 %gate_both.1 = (f32[512,1536]{1,0:T(8,128)}, bf16[512,1536]{1,0:T(8,128)(2,1)}, bf16[512,768]{1,0:T(8,128)(2,1)}, bf16[512,1536]{1,0:T(8,128)(2,1)}, bf16[512,15...) custom-call(f32[512,1536]{1,0:T(8,128)} %get-tuple-element.64.open_ref, ...), custom_call_target="tpu_custom_call" | custom-call | tf_op jit(solution)/shard_map/gate_both/pallas_call | solution.py:605
  125.7 3.0 convolution_convert_fusion.1
  128.7 2.6 fusion.106
  132.7 2.6 convolution_convert_fusion.2
  148.9 5.6 %collective-permute-done.17 = bf16[784,128]{1,0:T(8,128)(2,1)} collective-permute-done((bf16[784,128]{1,0:T(8,128)(2,1)}, bf16[784,128]{1,0:T(8,128)(2,1)}, u32[]{:S(2)}, u32[]{:S(2)}) %collective-permute-start.17) | collective-permute-done | bytes 200736 | tf_op jit(solution)/shard_map/ppermute | solution.py:133
  164.3 28.5 %scan_backward.1 = (f32[528,1536]{1,0:T(8,128)}, f32[8,1536]{1,0:T(8,128)}, f32[528,256]{1,0:T(8,128)}, f32[8,256]{1,0:T(8,128)}, f32[512,128]{1,0:T(8,128)}, /*index=5*/f32[512,128]{1,0:T(8,128)}) custom-call(bf16[512,1536]{1,0:T(8,128)(2,1)} %get-tuple-element.65.x_ref.refs_0_, bf16[528,1536]{1,0:T(8,128)(2,1)} %convolution_convert_fusion.3.mixed_ref.refs_1_, ...), custom_call_target="tpu_custom_call" | custom-call | tf_op jit(solution)/shard_map/scan_backward/pallas_call | solution.py:670
  221.0 2.9 fusion.6
  226.8 4.1 %collective-permute-done.24 = bf16[4,96,384]{2,1,0:T(8,128)(2,1)} collective-permute-done((bf16[4,96,384]{2,1,0:T(8,128)(2,1)}, bf16[4,96,384]{2,1,0:T(8,128)(2,1)}, u32[]{:S(2)}, u32[]{:S(2)}) %collective-permute-start.24) | collective-permute-done | bytes 294944 | tf_op jit(solution)/shard_map/ppermute | solution.py:28
  238.1 7.5 %collective-permute-done.32 = bf16[96,1920]{1,0:T(8,128)(2,1)S(1)} collective-permute-done((bf16[96,1920]{1,0:T(8,128)(2,1)S(1)}, bf16[96,1920]{1,0:T(8,128)(2,1)S(1)}, u32[]{:S(2)}, u32[]{:S(2)}) %collective-permute-start.32) | collective-permute-done | bytes 368672 | tf_op jit(solution)/shard_map/ppermute | solution.py:28
  247.6 3.7 %collective-permute-done.33 = bf16[48,1920]{1,0:T(8,128)(2,1)S(1)} collective-permute-done((bf16[48,1920]{1,0:T(8,128)(2,1)S(1)}, bf16[48,1920]{1,0:T(8,128)(2,1)S(1)}, u32[]{:S(2)}, u32[]{:S(2)}) %collective-permute-start.33) | collective-permute-done | bytes 184352 | tf_op jit(solution)/shard_map/ppermute | solution.py:28
  252.8 6.3 %collective-permute-done.36 = bf16[6,48,384]{2,1,0:T(8,128)(2,1)S(1)} collective-permute-done((bf16[6,48,384]{2,1,0:T(8,128)(2,1)S(1)}, bf16[6,48,384]{2,1,0:T(8,128)(2,1)S(1)}, u32[]{:S(2)}, u32[]{:S(2)}) %collective-permute-start.36) | collective-permute-done | bytes 221216 | tf_op jit(solution)/shard_map/ppermute | solution.py:28
  259.9 14.1 %collective-permute-done.37 = bf16[4,48,384]{2,1,0:T(8,128)(2,1)S(1)} collective-permute-done((bf16[4,48,384]{2,1,0:T(8,128)(2,1)S(1)}, bf16[4,48,384]{2,1,0:T(8,128)(2,1)S(1)}, u32[]{:S(2)}, u32[]{:S(2)}) %collective-permute-start.37) | collective-permute-done | bytes 147488 | tf_op jit(solution)/shard_map/ppermute | solution.py:28
  281.7 4.5 %collective-permute-done.39 = bf16[2,96,768]{2,1,0:T(8,128)(2,1)S(1)} collective-permute-done((bf16[2,96,768]{2,1,0:T(8,128)(2,1)S(1)}, bf16[2,96,768]{2,1,0:T(8,128)(2,1)S(1)}, u32[]{:S(2)}, u32[]{:S(2)}) %collective-permute-start.39) | collective-permute-done | bytes 294944 | tf_op jit(solution)/shard_map/ppermute | solution.py:28
  292.0 6.0 %collective-permute-done.29 = f32[96,128]{1,0:T(8,128)S(1)} collective-permute-done((f32[96,128]{1,0:T(8,128)S(1)}, f32[96,128]{1,0:T(8,128)S(1)}, u32[]{:S(2)}, u32[]{:S(2)}) %collective-permute-start.29) | collective-permute-done | bytes 49184 | tf_op jit(solution)/shard_map/ppermute | solution.py:28
  298.7 3.6 %collective-permute-start.30 = (f32[96,128]{1,0:T(8,128)}, f32[96,128]{1,0:T(8,128)}, u32[]{:S(2)}, u32[]{:S(2)}) collective-permute-start(f32[96,128]{1,0:T(8,128)} %add.451), channel_id=1, source_target_pairs={{0,2},{1,3},{2,0},{3,1},{4,6},{5,7},{6,4},{7,5},{8,10},{9,11},{10,... | collective-permute-start | bytes 147464 | tf_op jit(solution)/shard_map/ppermute | solution.py:28
  302.3 7.0 %collective-permute-done.30 = f32[96,128]{1,0:T(8,128)} collective-permute-done((f32[96,128]{1,0:T(8,128)}, f32[96,128]{1,0:T(8,128)}, u32[]{:S(2)}, u32[]{:S(2)}) %collective-permute-start.30) | collective-permute-done | bytes 49184 | tf_op jit(solution)/shard_map/ppermute | solution.py:28
  326.4 2.9 reshape.807
  334.5 6.4 %convert_add_fusion = f32[4,512,768]{2,1,0:T(8,128)} fusion(bf16[4,512,768]{2,1,0:T(8,128)(2,1)} %bitcast.241, bf16[4,512,768]{2,1,0:T(8,128)(2,1)} %param.33), kind=kLoop, calls=%fused_computation | loop fusion | flops 4718592 | bytes 12582912 | tf_op jit(solution)/shard_map/add | solution.py:905
  (449 shorter events, 168.9 us)
Async XLA Ops:
  7.2 78.8 %all-gather.7.cloned.1.call-start = ((), (), s32[]{:S(2)}) async-start(), calls=%async_computation | async-start | bytes 4866048 | tf_op jit(solution)/shard_map/all_gather | solution.py:753
  11.0 18.4 %collective-permute-start.1 = (bf16[128,384]{1,0:T(8,128)(2,1)S(1)}, bf16[128,384]{1,0:T(8,128)(2,1)S(1)}, u32[]{:S(2)}, u32[]{:S(2)}) collective-permute-start(bf16[128,384]{1,0:T(8,128)(2,1)S(1)} %pad_maximum_fusion.19), channel_id=1, source_target_pairs={{0,3},{1,0},{2,1},{3,2},{4,7},{5,4},{6,5},{7,6},{8,11},{9,8},{10,9... | collective-permute-start | bytes 294920 | tf_op jit(solution)/shard_map/ppermute | solution.py:61
  16.1 13.3 %collective-permute-start.2 = (bf16[128,384]{1,0:T(8,128)(2,1)S(1)}, bf16[128,384]{1,0:T(8,128)(2,1)S(1)}, u32[]{:S(2)}, u32[]{:S(2)}) collective-permute-start(bf16[128,384]{1,0:T(8,128)(2,1)S(1)} %pad_maximum_fusion.19), channel_id=1, source_target_pairs={{0,2},{1,3},{2,0},{3,1},{4,6},{5,7},{6,4},{7,5},{8,10},{9,11},{10,... | collective-permute-start | bytes 294920 | tf_op jit(solution)/shard_map/ppermute | solution.py:61
  16.1 13.4 %collective-permute-start.3 = (bf16[128,384]{1,0:T(8,128)(2,1)S(1)}, bf16[128,384]{1,0:T(8,128)(2,1)S(1)}, u32[]{:S(2)}, u32[]{:S(2)}) collective-permute-start(bf16[128,384]{1,0:T(8,128)(2,1)S(1)} %pad_maximum_fusion.19), channel_id=1, source_target_pairs={{0,1},{1,2},{2,3},{3,0},{4,5},{5,6},{6,7},{7,4},{8,9},{9,10},{10,1... | collective-permute-start | bytes 294920 | tf_op jit(solution)/shard_map/ppermute | solution.py:61
  17.8 9.9 %collective-permute-start = (bf16[16,768]{1,0:T(8,128)(2,1)S(1)}, bf16[16,768]{1,0:T(8,128)(2,1)S(1)}, u32[]{:S(2)}, u32[]{:S(2)}) collective-permute-start(bf16[16,768]{1,0:T(8,128)(2,1)S(1)} %dynamic-slice_bitcast_fusion.10), channel_id=1, source_target_pairs={{0,4},{1,5},{2,6},{3,7},{4,8},{5,9},{6,10},{7,11},{8,12},{9,13},{1... | collective-permute-start | bytes 73736 | tf_op jit(solution)/shard_map/ppermute | solution.py:133
  20.8 301.1 %all-gather.9.cloned.1.call-start = ((), (), s32[]{:S(2)}) async-start(), calls=%async_computation.1 | async-start | bytes 3932160 | tf_op jit(solution)/shard_map/all_gather | solution.py:842
  37.8 10.3 %collective-permute-start.5 = (bf16[96,1536]{1,0:T(8,128)(2,1)S(1)}, bf16[96,1536]{1,0:T(8,128)(2,1)S(1)}, u32[]{:S(2)}, u32[]{:S(2)}) collective-permute-start(bf16[96,1536]{1,0:T(8,128)(2,1)S(1)} %maximum_select_fusion.8), channel_id=1, source_target_pairs={{0,8},{4,12},{8,0},{12,4},{16,24},{20,28},{24,16},{28,20},{1,9},{5... | collective-permute-start | bytes 884744 | tf_op jit(solution)/shard_map/ppermute | solution.py:28
  82.7 11.7 %collective-permute-start.10 = (bf16[784,128]{1,0:T(8,128)(2,1)}, bf16[784,128]{1,0:T(8,128)(2,1)S(1)}, u32[]{:S(2)}, u32[]{:S(2)}) collective-permute-start(bf16[784,128]{1,0:T(8,128)(2,1)} %pad_maximum_fusion.11), channel_id=1, source_target_pairs={{0,8},{1,9},{2,10},{3,11},{4,12},{5,13},{6,14},{7,15},{8,0},{9,1},... | collective-permute-start | bytes 602120 | tf_op jit(solution)/shard_map/ppermute | solution.py:133
  97.4 10.9 %collective-permute-start.11 = (bf16[784,128]{1,0:T(8,128)(2,1)}, bf16[784,128]{1,0:T(8,128)(2,1)}, u32[]{:S(2)}, u32[]{:S(2)}) collective-permute-start(bf16[784,128]{1,0:T(8,128)(2,1)} %pad_maximum_fusion.12), channel_id=1, source_target_pairs={{0,16},{1,17},{2,18},{3,19},{4,20},{5,21},{6,22},{7,23},{8,24},{9,... | collective-permute-start | bytes 602120 | tf_op jit(solution)/shard_map/ppermute | solution.py:133
  159.1 33.8 %collective-permute-start.20 = (bf16[192,1536]{1,0:T(8,128)(2,1)S(1)}, bf16[192,1536]{1,0:T(8,128)(2,1)}, u32[]{:S(2)}, u32[]{:S(2)}) collective-permute-start(bf16[192,1536]{1,0:T(8,128)(2,1)S(1)} %constant_dynamic-slice_fusion.14), channel_id=1, source_target_pairs={{0,16},{4,20},{8,24},{12,28},{16,0},{20,4},{24,8},{28,12},{1,17},{... | collective-permute-start | bytes 1769480 | tf_op jit(solution)/shard_map/ppermute | solution.py:28
  161.2 32.9 %collective-permute-start.19 = (bf16[192,1536]{1,0:T(8,128)(2,1)}, bf16[192,1536]{1,0:T(8,128)(2,1)}, u32[]{:S(2)}, u32[]{:S(2)}) collective-permute-start(bf16[192,1536]{1,0:T(8,128)(2,1)} %constant_dynamic-slice_fusion.15), channel_id=1, source_target_pairs={{0,8},{4,12},{8,0},{12,4},{16,24},{20,28},{24,16},{28,20},{1,9},{5... | collective-permute-start | bytes 1769480 | tf_op jit(solution)/shard_map/ppermute | solution.py:28
  164.3 170.2 %all-gather.11.cloned.1.call-start = ((), (), s32[]{:S(2)}) async-start(), calls=%async_computation.2 | async-start | bytes 3932160 | tf_op jit(solution)/shard_map/all_gather | solution.py:904
  197.4 10.4 %collective-permute-start.23 = (bf16[96,1536]{1,0:T(8,128)(2,1)}, bf16[96,1536]{1,0:T(8,128)(2,1)S(1)}, u32[]{:S(2)}, u32[]{:S(2)}) collective-permute-start(bf16[96,1536]{1,0:T(8,128)(2,1)} %constant_dynamic-slice_fusion.12), channel_id=1, source_target_pairs={{0,8},{4,12},{8,0},{12,4},{16,24},{20,28},{24,16},{28,20},{1,9},{5... | collective-permute-start | bytes 884744 | tf_op jit(solution)/shard_map/ppermute | solution.py:28
  212.5 11.4 %collective-permute-start.31 = (bf16[2,192,1920]{2,1,0:T(8,128)(2,1)}, bf16[2,192,1920]{2,1,0:T(8,128)(2,1)}, u32[]{:S(2)}, u32[]{:S(2)}) collective-permute-start(bf16[2,192,1920]{2,1,0:T(8,128)(2,1)} %constant_dynamic-slice_fusion.9), channel_id=1, source_target_pairs={{0,4},{4,0},{8,12},{12,8},{16,20},{20,16},{24,28},{28,24},{1,5},{5... | collective-permute-start | bytes 4423688 | tf_op jit(solution)/shard_map/ppermute | solution.py:28
  214.7 16.3 %collective-permute-start.24 = (bf16[4,96,384]{2,1,0:T(8,128)(2,1)}, bf16[4,96,384]{2,1,0:T(8,128)(2,1)}, u32[]{:S(2)}, u32[]{:S(2)}) collective-permute-start(bf16[4,96,384]{2,1,0:T(8,128)(2,1)} %bitcast.49), channel_id=1, source_target_pairs={{0,1},{1,0},{2,3},{3,2},{4,5},{5,4},{6,7},{7,6},{8,9},{9,8},{10,11... | collective-permute-start | bytes 884744 | tf_op jit(solution)/shard_map/ppermute | solution.py:28
  221.0 53.4 %collective-permute-start.26 = (f32[96,128]{1,0:T(8,128)}, f32[96,128]{1,0:T(8,128)}, u32[]{:S(2)}, u32[]{:S(2)}) collective-permute-start(f32[96,128]{1,0:T(8,128)} %pad_bitcast_fusion), channel_id=1, source_target_pairs={{0,4},{4,0},{8,12},{12,8},{16,20},{20,16},{24,28},{28,24},{1,5},{5... | collective-permute-start | bytes 147464 | tf_op jit(solution)/shard_map/ppermute | solution.py:28
  225.8 11.1 %collective-permute-start.34 = (bf16[96,1920]{1,0:T(8,128)(2,1)S(1)}, bf16[96,1920]{1,0:T(8,128)(2,1)S(1)}, u32[]{:S(2)}, u32[]{:S(2)}) collective-permute-start(bf16[96,1920]{1,0:T(8,128)(2,1)S(1)} %dynamic-slice_bitcast_fusion.1), channel_id=1, source_target_pairs={{0,16},{4,20},{8,24},{12,28},{16,0},{20,4},{24,8},{28,12},{1,17},{... | collective-permute-start | bytes 1105928 | tf_op jit(solution)/shard_map/ppermute | solution.py:28
  232.0 20.7 %collective-permute-start.25 = (bf16[2,96,384]{2,1,0:T(8,128)(2,1)S(1)}, bf16[2,96,384]{2,1,0:T(8,128)(2,1)S(1)}, u32[]{:S(2)}, u32[]{:S(2)}) collective-permute-start(bf16[2,96,384]{2,1,0:T(8,128)(2,1)S(1)} %dynamic-slice_bitcast_fusion.3), channel_id=1, source_target_pairs={{0,2},{1,3},{2,0},{3,1},{4,6},{5,7},{6,4},{7,5},{8,10},{9,11},{10,... | collective-permute-start | bytes 442376 | tf_op jit(solution)/shard_map/ppermute | solution.py:28
  234.2 11.4 %collective-permute-start.32 = (bf16[96,1920]{1,0:T(8,128)(2,1)S(1)}, bf16[96,1920]{1,0:T(8,128)(2,1)S(1)}, u32[]{:S(2)}, u32[]{:S(2)}) collective-permute-start(bf16[96,1920]{1,0:T(8,128)(2,1)S(1)} %dynamic-slice_bitcast_fusion.2), channel_id=1, source_target_pairs={{0,8},{4,12},{8,0},{12,4},{16,24},{20,28},{24,16},{28,20},{1,9},{5... | collective-permute-start | bytes 1105928 | tf_op jit(solution)/shard_map/ppermute | solution.py:28
  237.0 10.5 %collective-permute-start.35 = (bf16[48,1920]{1,0:T(8,128)(2,1)S(1)}, bf16[48,1920]{1,0:T(8,128)(2,1)S(1)}, u32[]{:S(2)}, u32[]{:S(2)}) collective-permute-start(bf16[48,1920]{1,0:T(8,128)(2,1)S(1)} %constant_dynamic-slice_fusion.7), channel_id=1, source_target_pairs={{0,8},{4,12},{8,0},{12,4},{16,24},{20,28},{24,16},{28,20},{1,9},{5... | collective-permute-start | bytes 552968 | tf_op jit(solution)/shard_map/ppermute | solution.py:28
  259.3 14.8 %collective-permute-start.37 = (bf16[4,48,384]{2,1,0:T(8,128)(2,1)S(1)}, bf16[4,48,384]{2,1,0:T(8,128)(2,1)S(1)}, u32[]{:S(2)}, u32[]{:S(2)}) collective-permute-start(bf16[4,48,384]{2,1,0:T(8,128)(2,1)S(1)} %pad_maximum_fusion.15), channel_id=1, source_target_pairs={{0,2},{1,3},{2,0},{3,1},{4,6},{5,7},{6,4},{7,5},{8,10},{9,11},{10,... | collective-permute-start | bytes 442376 | tf_op jit(solution)/shard_map/ppermute | solution.py:28
  275.2 11.4 %collective-permute-start.27 = (f32[96,128]{1,0:T(8,128)S(1)}, f32[96,128]{1,0:T(8,128)S(1)}, u32[]{:S(2)}, u32[]{:S(2)}) collective-permute-start(f32[96,128]{1,0:T(8,128)S(1)} %fusion.96), channel_id=1, source_target_pairs={{0,8},{4,12},{8,0},{12,4},{16,24},{20,28},{24,16},{28,20},{1,9},{5... | collective-permute-start | bytes 147464 | tf_op jit(solution)/shard_map/ppermute | solution.py:28
  286.6 35.3 %collective-permute-start.42 = (bf16[4,2,96,768]{3,2,0,1:T(8,128)(2,1)S(1)}, bf16[4,2,96,768]{3,2,0,1:T(8,128)(2,1)S(1)}, u32[]{:S(2)}, u32[]{:S(2)}) collective-permute-start(bf16[4,2,96,768]{3,2,0,1:T(8,128)(2,1)S(1)} %pad_maximum_fusion.2), channel_id=1, source_target_pairs={{0,4},{4,0},{8,12},{12,8},{16,20},{20,16},{24,28},{28,24},{1,5},{5... | collective-permute-start | bytes 3538952 | tf_op jit(solution)/shard_map/ppermute | solution.py:28
  298.7 10.6 %collective-permute-start.30 = (f32[96,128]{1,0:T(8,128)}, f32[96,128]{1,0:T(8,128)}, u32[]{:S(2)}, u32[]{:S(2)}) collective-permute-start(f32[96,128]{1,0:T(8,128)} %add.451), channel_id=1, source_target_pairs={{0,2},{1,3},{2,0},{3,1},{4,6},{5,7},{6,4},{7,5},{8,10},{9,11},{10,... | collective-permute-start | bytes 147464 | tf_op jit(solution)/shard_map/ppermute | solution.py:28
  (68 other events, 337.8 us)
Sparse Core Ops, SparseCore 0:
  20.9 65.0 all-gather.6
  164.4 64.1 all-gather.8
  252.9 67.4 all-gather.10
